TPU v7x, 512 devices: a whole 4x8x8 slice. The times are simulated.
512 devices in a mesh: resp: 8 (over y_lo, core), tp: 16 (over y_hi, z), grp: 4 (over x).
Axes of the slice: x: 4, y: 8 (y_hi: 2, y_lo: 4; y = y_hi * 4 + y_lo), z: 8, core: 2. Of those that a mesh axis runs over, the one named last changes fastest.
Arguments:
- queries: bfloat16 [4096, 8192], P(('grp', 'resp'), 'tp'), parts along dimension 0, may hold values from -8 to 8
- resp_keys: bfloat16 [4096, 1024], P(('grp', 'resp')), parts along dimension 0, may hold values from -6 to 6
- resp_values: bfloat16 [4096, 1024], P(('grp', 'resp')), parts along dimension 0, may hold values from -6 to 6
- prefix_keys: bfloat16 [8192, 1024], P(('grp', 'resp', 'tp')), parts along dimension 0, may hold values from -8 to 8
- prefix_values: bfloat16 [8192, 1024], P(('grp', 'resp', 'tp')), parts along dimension 0, may hold values from -6 to 6
- cotangent: bfloat16 [4096, 8192], P(('grp', 'resp'), 'tp'), parts along dimension 0, may hold values from -96 to 96
- lengths: int32 [32], P('grp'), parts along dimension 0, may hold values from 1 to 128, 640 in all
Outputs:
- resp_dq: float32 [4096, 8192], P(('grp', 'resp'), 'tp'), parts along dimension 0
- resp_dk: float32 [4096, 1024], P(('grp', 'resp', 'tp')), parts along dimension 0
- resp_dv: float32 [4096, 1024], P(('grp', 'resp', 'tp')), parts along dimension 0
- prefix_dk: float32 [8192, 1024], P(('grp', 'tp'), 'resp'), parts along dimension 0
- prefix_dv: float32 [8192, 1024], P(('grp', 'tp'), 'resp'), parts along dimension 0
There are 4 independent parts, one for each index of `grp`. A program takes and returns all parts, laid end to end along the dimension named above; each array names one. Nothing has to cross between parts.
All inputs are finite; a program needn't handle non-finite values.
Results may differ from a plain program's by a relative error of at most 0.0074.
Values may be sent and summed in bfloat16 or wider, within the bound.
A program may use at most 64 MiB of HBM per device.

v0:
```python
import math

import jax
import jax.numpy as jnp
from jax import lax
from jax.sharding import PartitionSpec as P

KVH = 8
HD = 128


def block_grads(query_block, dout_block, keys, values, prefix):
    scale = 1.0 / math.sqrt(query_block.shape[3])
    count = query_block.shape[0]
    total = keys.shape[0]
    scores = (
        jnp.einsum("rkgd,skd->kgrs", query_block, keys, preferred_element_type=jnp.float32) * scale
    )
    row_pos = lax.broadcasted_iota(jnp.int32, (count, total), 0)
    col_pos = lax.broadcasted_iota(jnp.int32, (count, total), 1)
    allowed = (col_pos < prefix) | (col_pos - prefix <= row_pos)
    scores = jnp.where(allowed, scores, -jnp.inf)
    top = jnp.max(scores, axis=3, keepdims=True)
    expo = jnp.exp(scores - top)
    probs = expo / jnp.sum(expo, axis=3, keepdims=True)
    probs_b = probs.astype(jnp.bfloat16)
    attended = jnp.einsum("kgrs,skd->kgrd", probs_b, values, preferred_element_type=jnp.float32)
    d_prob = jnp.einsum("rkgd,skd->kgrs", dout_block, values, preferred_element_type=jnp.float32)
    dout_rows = jnp.transpose(dout_block.astype(jnp.float32), (1, 2, 0, 3))
    delta = jnp.sum(dout_rows * attended, axis=3, keepdims=True)
    d_score = (probs * (d_prob - delta)).astype(jnp.bfloat16)
    grad_query = (
        jnp.einsum("kgrs,skd->rkgd", d_score, keys, preferred_element_type=jnp.float32) * scale
    )
    grad_key = (
        jnp.einsum("kgrs,rkgd->skd", d_score, query_block, preferred_element_type=jnp.float32)
        * scale
    )
    grad_value = jnp.einsum(
        "kgrs,rkgd->skd", probs_b, dout_block, preferred_element_type=jnp.float32
    )
    return (grad_query, grad_key, grad_value)


def take_columns(source, start, width):
    return lax.dynamic_slice_in_dim(source, start, width, 1)


def fold_copies(source, share):
    return jnp.sum(source.reshape(source.shape[0], KVH, share, HD), axis=2).reshape(
        source.shape[0], KVH * HD
    )


def per_device(queries, resp_keys, resp_values, prefix_keys, prefix_values, cotangent, lengths):
    n_heads_axis = lax.axis_size("tp")
    kv_local = max(1, KVH // n_heads_axis)
    share = max(1, n_heads_axis // KVH)
    width = kv_local * HD
    count = queries.shape[0]
    group = queries.shape[1] // width
    col_start = lax.axis_index("tp") // share * width
    length = lax.dynamic_index_in_dim(lengths, lax.axis_index("resp"), 0, keepdims=False)
    all_keys, all_values = (
        lax.all_gather(prefix_keys, ("resp", "tp"), axis=0, tiled=True),
        lax.all_gather(prefix_values, ("resp", "tp"), axis=0, tiled=True),
    )
    pre_keys = take_columns(all_keys, col_start, width)
    pre_values = take_columns(all_values, col_start, width)
    prefix = pre_keys.shape[0]
    keys = jnp.concatenate([pre_keys, take_columns(resp_keys, col_start, width)], 0).reshape(
        prefix + count, kv_local, HD
    )
    values = jnp.concatenate([pre_values, take_columns(resp_values, col_start, width)], 0).reshape(
        prefix + count, kv_local, HD
    )
    live = lax.broadcasted_iota(jnp.int32, cotangent.shape, 0) < length
    masked = jnp.where(live, cotangent, jnp.zeros_like(cotangent))
    query_all = queries.reshape(count, kv_local, group, HD)
    dout_all = masked.reshape(count, kv_local, group, HD)
    limit = max(1, min(8, kv_local * group * count // 512))
    n_blocks = 1
    while n_blocks * 2 <= limit and count % (n_blocks * 2) == 0:
        n_blocks = n_blocks * 2
    block_query, block_key, block_value = block_grads(query_all, dout_all, keys, values, prefix)
    resp_dq = block_query.reshape(count, kv_local * group * HD)
    flat_keys = block_key.reshape(prefix + count, width)
    flat_values = block_value.reshape(prefix + count, width)
    moved = (
        lax.all_to_all(flat_keys[:prefix], "tp", split_axis=0, concat_axis=1, tiled=True),
        lax.all_to_all(flat_values[:prefix], "tp", split_axis=0, concat_axis=1, tiled=True),
        lax.all_to_all(flat_keys[prefix:], "tp", split_axis=0, concat_axis=1, tiled=True),
        lax.all_to_all(flat_values[prefix:], "tp", split_axis=0, concat_axis=1, tiled=True),
    )
    prefix_dk, prefix_dv = (
        lax.psum_scatter(fold_copies(moved[0], share), "resp", scatter_dimension=1, tiled=True),
        lax.psum_scatter(fold_copies(moved[1], share), "resp", scatter_dimension=1, tiled=True),
    )
    resp_dk = fold_copies(moved[2], share)
    resp_dv = fold_copies(moved[3], share)
    return (resp_dq, resp_dk, resp_dv, prefix_dk, prefix_dv)


def solution(mesh):
    placed = (
        P(("grp", "resp"), "tp"),
        P(("grp", "resp"), None),
        P(("grp", "resp"), None),
        P(("grp", "resp", "tp"), None),
        P(("grp", "resp", "tp"), None),
        P(("grp", "resp"), "tp"),
        P("grp"),
    )
    return jax.shard_map(
        per_device,
        mesh=mesh,
        in_specs=placed,
        out_specs=(
            P(("grp", "resp"), "tp"),
            P(("grp", "resp", "tp"), None),
            P(("grp", "resp", "tp"), None),
            P(("grp", "tp"), "resp"),
            P(("grp", "tp"), "resp"),
        ),
        check_vma=False,
    )
```

profile of v0, /device:TPU:1, one launch (start us, length us, event | category | flops | bytes accessed | tf_op | source)
XLA Modules:
  0.0 906.3 jit_solution(11581350205144570069)
XLA Ops:
  8.7 1.2 dynamic_slice.20
  12.6 1.5 fusion.23
  14.2 366.5 %all-gather.3.cloned.1.call-done = bf16[2048,1024]{1,0:T(8,128)(2,1)} async-done(((bf16[16,1024]{1,0:T(8,128)(2,1)}), bf16[2048,1024]{1,0:T(8,128)(2,1)}) %all-gather.3.cloned.1.call-update) | async-done | bytes 4194320 | tf_op jit(solution)/shard_map/all_gather | solution.py:65
  383.2 1.4 copy-done.1
  385.4 365.1 %all-gather.5.cloned.1.call-done = bf16[2048,1024]{1,0:T(8,128)(2,1)} async-done(((bf16[16,1024]{1,0:T(8,128)(2,1)}), bf16[2048,1024]{1,0:T(8,128)(2,1)}) %all-gather.5.cloned.1.call-update) | async-done | bytes 4194320 | tf_op jit(solution)/shard_map/all_gather | solution.py:66
  750.5 1.2 constant_dynamic-slice_fusion.1
  753.0 1.1 fusion.5
  756.0 13.9 %all-to-all-start.2 = ((f32[16,128,128]{2,1,0:T(8,128)}), f32[16,128,128]{2,1,0:T(8,128)}, u32[]{:S(2)}, u32[]{:S(2)}) async-start(f32[16,128,128]{2,1,0:T(8,128)} %bitcast.124), calls=%async_computation.2 | async-start | bytes 2097152 | tf_op jit(solution)/shard_map/all_to_all | solution.py:90
  769.9 2.5 convolution_bitcast_fusion.1
  773.7 1.3 copy.61
  775.0 24.1 %all-to-all-done.2 = f32[16,128,128]{2,1,0:T(8,128)} async-done(((f32[16,128,128]{2,1,0:T(8,128)}), f32[16,128,128]{2,1,0:T(8,128)}, u32[]{:S(2)}, u32[]{:S(2)}) %all-to-all-start.2) | async-done | bytes 1048608 | tf_op jit(solution)/shard_map/all_to_all | solution.py:90
  799.2 7.8 all-to-all-start.3
  807.0 2.2 bitcast_reduce_fusion.1
  809.1 2.1 copy.60
  811.3 24.0 %all-to-all-done.3 = f32[16,128,128]{1,2,0:T(8,128)} async-done(((f32[16,128,128]{1,2,0:T(8,128)}), f32[16,128,128]{1,2,0:T(8,128)}, u32[]{:S(2)}, u32[]{:S(2)}) %all-to-all-start.3) | async-done | bytes 1048608 | tf_op jit(solution)/shard_map/all_to_all | solution.py:91
  835.3 2.2 bitcast_reduce_fusion
  838.1 7.5 all-to-all-start
  846.4 10.6 %all-to-all-done = f32[16,8,128]{2,1,0:T(8,128)S(1)} async-done(((f32[16,8,128]{2,1,0:T(8,128)}), f32[16,8,128]{2,1,0:T(8,128)S(1)}, u32[]{:S(2)}, u32[]{:S(2)}) %all-to-all-start) | async-done | bytes 65568 | tf_op jit(solution)/shard_map/all_to_all | solution.py:92
  856.9 3.5 all-to-all-start.1
  860.5 1.6 convolution_multiply_fusion.1
  863.5 8.2 all-to-all-done.1
  872.3 1.6 copy.65
  873.9 24.4 %reduce-scatter.5.cloned.1.call-done = f32[128,128]{0,1:T(8,128)} async-done(((f32[128,1024]{0,1:T(8,128)}), f32[128,128]{0,1:T(8,128)}) %reduce-scatter.5.cloned.1.call-update) | async-done | bytes 65552 | tf_op jit(solution)/shard_map/reduce_scatter | solution.py:97
  898.2 1.6 copy.66
  (47 shorter events, 15.2 us)
Async XLA Ops:
  7.2 374.6 %copy-start = (bf16[128,512]{1,0:T(8,128)(2,1)S(1)}, bf16[128,512]{1,0:T(8,128)(2,1)}, u32[]{:S(2)}) copy-start(bf16[128,512]{1,0:T(8,128)(2,1)} %param.7) | copy-start | bytes 393220
  7.2 373.5 %all-gather.3.cloned.1.call-start = ((), (), s32[]{:S(2)}) async-start(), calls=%async_computation.6 | async-start | bytes 4227072 | tf_op jit(solution)/shard_map/all_gather | solution.py:65
  7.9 742.6 %all-gather.5.cloned.1.call-start = ((), (), s32[]{:S(2)}) async-start(), calls=%async_computation.7 | async-start | bytes 4227072 | tf_op jit(solution)/shard_map/all_gather | solution.py:66
  11.7 740.6 %copy-start.6 = (bf16[128,512]{0,1:T(8,128)(2,1)}, bf16[128,512]{0,1:T(8,128)(2,1)S(1)}, u32[]{:S(2)}) copy-start(bf16[128,512]{0,1:T(8,128)(2,1)S(1)} %copy.75) | copy-start | bytes 393220
  12.6 369.9 %copy-start.7 = (bf16[128,128]{1,0:T(8,128)(2,1)}, bf16[128,128]{1,0:T(8,128)(2,1)S(1)}, u32[]{:S(2)}) copy-start(bf16[128,128]{1,0:T(8,128)(2,1)S(1)} %get-tuple-element.28) | copy-start | bytes 98308
  381.8 0.8 copy-start.5
  382.6 2.0 copy-start.1
  385.4 367.0 %copy-start.3 = (bf16[1,4,128,2176]{2,3,1,0:T(8,128)(2,1)}, bf16[1,4,128,2176]{2,3,1,0:T(8,128)(2,1)S(1)}, u32[]{:S(2)}) copy-start(bf16[1,4,128,2176]{2,3,1,0:T(8,128)(2,1)S(1)} %fusion.13) | copy-start | bytes 6684676
  750.5 2.4 copy-start.2
  756.0 43.2 %all-to-all-start.2 = ((f32[16,128,128]{2,1,0:T(8,128)}), f32[16,128,128]{2,1,0:T(8,128)}, u32[]{:S(2)}, u32[]{:S(2)}) async-start(f32[16,128,128]{2,1,0:T(8,128)} %bitcast.124), calls=%async_computation.2 | async-start | bytes 2097152 | tf_op jit(solution)/shard_map/all_to_all | solution.py:90
  772.5 1.0 copy-start.4
  799.2 36.2 %all-to-all-start.3 = ((f32[16,128,128]{1,2,0:T(8,128)}), f32[16,128,128]{1,2,0:T(8,128)}, u32[]{:S(2)}, u32[]{:S(2)}) async-start(f32[16,128,128]{1,2,0:T(8,128)} %copy.61), calls=%async_computation.4 | async-start | bytes 2097152 | tf_op jit(solution)/shard_map/all_to_all | solution.py:91
  806.9 65.4 %reduce-scatter.3.cloned.1.call-start = ((), (), s32[]{:S(2)}) async-start(), calls=%async_computation.8 | async-start | bytes 589824 | tf_op jit(solution)/shard_map/reduce_scatter | solution.py:96
  809.1 36.5 %slice-start = ((f32[2176,1,128]{0,2,1:T(8,128)}), f32[128,1,128]{0,2,1:T(8,128)S(1)}, s32[]{:S(2)}) async-start(f32[2176,1,128]{0,2,1:T(8,128)} %copy-done.4), calls=%async_computation.10 | async-start | bytes 131072 | tf_op jit(solution)/shard_map/slice | solution.py:93
  811.2 87.0 %reduce-scatter.5.cloned.1.call-start = ((), (), s32[]{:S(2)}) async-start(), calls=%async_computation.9 | async-start | bytes 589824 | tf_op jit(solution)/shard_map/reduce_scatter | solution.py:97
  838.1 18.8 %all-to-all-start = ((f32[16,8,128]{2,1,0:T(8,128)}), f32[16,8,128]{2,1,0:T(8,128)S(1)}, u32[]{:S(2)}, u32[]{:S(2)}) async-start(f32[16,8,128]{2,1,0:T(8,128)} %slice_bitcast_fusion.1), calls=%async_computation | async-start | bytes 131072 | tf_op jit(solution)/shard_map/all_to_all | solution.py:92
  856.9 14.7 %all-to-all-start.1 = ((f32[16,8,128]{2,1,0:T(8,128)}), f32[16,8,128]{2,1,0:T(8,128)S(1)}, u32[]{:S(2)}, u32[]{:S(2)}) async-start(f32[16,8,128]{2,1,0:T(8,128)} %bitcast.28), calls=%async_computation.1 | async-start | bytes 131072 | tf_op jit(solution)/shard_map/all_to_all | solution.py:93
Sparse Core Ops, SparseCore 0:
  10.1 370.5 all-gather.2
  382.8 367.6 all-gather.4
  811.3 45.7 reduce-scatter.2
  860.0 38.2 reduce-scatter.4
where the time goes:
time: 909 us; the launch traced here: 906 us
  waiting for transfers between devices  824 us (91%)
  starting transfers between devices  32.8 us (4%)
  local copies, waits for them, and re-layouts  17.7 us (2%)
  between operations  14 us (2%)
  other arithmetic  10.1 us (1%)
    all_gather x1, waiting for transfers between devices, per_device(): lax.all_gather(prefix_keys, ('resp', 'tp'), axis=0, tiled=True)  367 us
    all_gather x1, waiting for transfers between devices, per_device(): lax.all_gather(prefix_values, ('resp', 'tp'), axis=0, tiled=True)  365 us
    reduce_scatter x1, waiting for transfers between devices, per_device(): lax.psum_scatter(fold_copies(moved[1], share), 'resp', scatter_dimension=...  24.4 us
    all_to_all x1, waiting for transfers between devices, per_device(): lax.all_to_all(flat_keys[:prefix], 'tp', split_axis=0, concat_axis=1, til...  24.1 us
    all_to_all x1, waiting for transfers between devices, per_device(): lax.all_to_all(flat_values[:prefix], 'tp', split_axis=0, concat_axis=1, t...  24 us
  transfers between devices with their start and end apart: 8, of which 7 were waited for; matrix products, arithmetic and copies ran while one was open for 3% of the time, Pallas kernels for 0%

commit v1 on v0

v1 whole, which is shorter than its diff:
```python
import functools
import math

import jax
import jax.numpy as jnp
from jax import lax
from jax.experimental import pallas as pl
from jax.experimental.pallas import tpu as pltpu
from jax.sharding import PartitionSpec as P

MESH = pl.DeviceIdType.MESH
HD = 128
CHUNK = 128
F32 = jnp.float32
BF16 = jnp.bfloat16


def flip(value, bits):
    if bits & 1:
        value = value + 1 - 2 * lax.rem(value, 2)
    if bits & 2:
        value = value + 2 - 4 * lax.rem(value // 2, 2)
    return value


def fold(x, op):
    return op(x.reshape(x.shape[0] // 8, 8, x.shape[1]), axis=0)


def kernel(
    n_resp,
    n_tp,
    q_hbm,
    rk_hbm,
    rv_hbm,
    pk_hbm,
    pv_hbm,
    ct_hbm,
    len_ref,
    dq_ref,
    rdk_ref,
    rdv_ref,
    pdk_ref,
    pdv_ref,
    pin,
    kv,
    rkv,
    q_s,
    do_s,
    q_t,
    do_t,
    st,
    dp,
    pb,
    st_r,
    dp_r,
    pb_r,
    mx,
    sm,
    dl,
    sib_send,
    sib_recv,
    acc,
    z_send,
    z_recv,
    y_send,
    y_recv,
    p_send,
    p_recv,
    rg_send,
    rg_recv,
    rg_acc,
    in_sem,
    a_send,
    a_recv,
    gy_send,
    gy_recv,
    gz_send,
    gz_recv,
    gs_send,
    gs_recv,
    fs_send,
    fs_recv,
    fz_send,
    fz_recv,
    fy_send,
    fy_recv,
    fp_send,
    fp_recv,
    rg_ssem,
    rg_rsem,
):
    r = lax.axis_index("resp")
    t = lax.axis_index("tp")
    n_y = n_resp // 2
    y, c = r // 2, lax.rem(r, 2)
    g, h = t // 2, lax.rem(t, 2)
    count = q_hbm.shape[0]
    heads = q_hbm.shape[1] // HD
    scale = 1.0 / math.sqrt(HD)
    block = kv.shape[2]
    half = block // 2

    sibling = {"resp": flip(r, 1), "tp": t}
    zpair = {"resp": r, "tp": flip(t, 1)}

    def yline(k):
        return {"resp": 2 * flip(y, k) + c, "tp": t}

    owner = {"resp": g, "tp": 2 * r + h}
    away = jnp.logical_not(r == g)

    def rcopy(src, dst, send, recv, dev):
        return pltpu.make_async_remote_copy(
            src_ref=src, dst_ref=dst, send_sem=send, recv_sem=recv, device_id=dev, device_id_type=MESH
        )

    col = pl.multiple_of(g * HD, HD)
    loads = [
        pltpu.make_async_copy(pk_hbm, pin.at[0], in_sem.at[0]),
        pltpu.make_async_copy(pv_hbm, pin.at[1], in_sem.at[1]),
        pltpu.make_async_copy(rk_hbm.at[:, pl.ds(col, HD)], rkv.at[0], in_sem.at[2]),
        pltpu.make_async_copy(rv_hbm.at[:, pl.ds(col, HD)], rkv.at[1], in_sem.at[3]),
    ]
    for j in range(heads):
        rows = pl.ds(j * count, count)
        loads.append(pltpu.make_async_copy(q_hbm.at[:, pl.ds(j * HD, HD)], q_s.at[rows], in_sem.at[4 + j]))
        loads.append(
            pltpu.make_async_copy(ct_hbm.at[:, pl.ds(j * HD, HD)], do_s.at[rows], in_sem.at[4 + heads + j])
        )
    for load in loads:
        load.start()

    barrier = pltpu.get_barrier_semaphore()

    def greet(d, carry):
        pl.semaphore_signal(
            barrier, inc=1, device_id={"resp": r, "tp": lax.rem(t + d, n_tp)}, device_id_type=MESH
        )
        return carry

    lax.fori_loop(1, n_tp, greet, 0)
    pl.semaphore_signal(barrier, inc=1, device_id=sibling, device_id_type=MESH)
    for k in range(1, n_y):
        pl.semaphore_signal(barrier, inc=1, device_id=yline(k), device_id_type=MESH)

    @pl.when(away)
    def _():
        pl.semaphore_signal(barrier, inc=1, device_id=owner, device_id_type=MESH)

    pl.semaphore_wait(barrier, n_tp - 1 + n_y + away.astype(jnp.int32))

    rows16 = pl.ds(pl.multiple_of(t * 16, 16), 16)
    for a in range(2):
        loads[a].wait()

        def scatter(d, carry, a=a):
            to = lax.rem(t + d, n_tp)
            rcopy(
                pin.at[a, :, pl.ds(pl.multiple_of((to // 2) * HD, HD), HD)],
                kv.at[a, r, rows16],
                a_send.at[a],
                a_recv.at[a],
                {"resp": r, "tp": to},
            ).start()
            return carry

        lax.fori_loop(1, n_tp, scatter, 0)
        pltpu.make_async_copy(pin.at[a, :, pl.ds(col, HD)], kv.at[a, r, rows16], a_recv.at[a]).start()

    for load in loads[2:]:
        load.wait()
    q_t[...] = jnp.transpose(q_s[...].astype(F32)).astype(BF16)
    length = len_ref[r]
    live = lax.rem(lax.broadcasted_iota(jnp.int32, do_s.shape, 0), count) < length
    masked = jnp.where(live, do_s[...].astype(F32), 0.0)
    do_s[...] = masked.astype(BF16)
    do_t[...] = jnp.transpose(masked).astype(BF16)

    s = jnp.dot(rkv[0], q_t[...], preferred_element_type=F32) * scale
    key_pos = lax.broadcasted_iota(jnp.int32, s.shape, 0)
    row_pos = lax.rem(lax.broadcasted_iota(jnp.int32, s.shape, 1), count)
    s = jnp.where(key_pos <= row_pos, s, -jnp.inf)
    st_r[...] = s
    mx[...] = fold(s, jnp.max)

    def mine(k):
        return 2 * flip(y, k) + c

    def other(k):
        return 2 * flip(y, k) + 1 - c

    own_half = pl.ds(pl.multiple_of(h * half, half), half)
    far_half = pl.ds(pl.multiple_of((1 - h) * half, half), half)

    sends = []

    def start(copy):
        copy.start()
        sends.append(copy)

    def gather_first(a):
        pltpu.make_async_copy(kv.at[a, r], kv.at[a, r], a_recv.at[a]).wait()
        for k in range(n_y - 1, 0, -1):
            ref = kv.at[a, r, own_half]
            start(rcopy(ref, ref, gy_send.at[a, k], gy_recv.at[a, k], yline(k)))
        start(rcopy(kv.at[a, r], kv.at[a, r], gs_send.at[a, 0, 0], gs_recv.at[a, 0, 0], sibling))

    def gather_y(a, k):
        ref = kv.at[a, mine(k), own_half]
        rcopy(ref, ref, gy_send.at[a, k], gy_recv.at[a, k], yline(k)).wait_recv()
        start(rcopy(ref, ref, gz_send.at[a, k], gz_recv.at[a, k], zpair))
        start(rcopy(ref, ref, gs_send.at[a, k, 0], gs_recv.at[a, k, 0], sibling))

    def gather_z(a, k):
        ref = kv.at[a, mine(k), far_half]
        rcopy(ref, ref, gz_send.at[a, k], gz_recv.at[a, k], zpair).wait_recv()
        start(rcopy(ref, ref, gs_send.at[a, k, 1], gs_recv.at[a, k, 1], sibling))

    def gather_sib(a, k):
        if k == 0:
            ref = kv.at[a, other(0)]
            rcopy(ref, ref, gs_send.at[a, 0, 0], gs_recv.at[a, 0, 0], sibling).wait_recv()
            return
        for i, part in enumerate((own_half, far_half)):
            ref = kv.at[a, other(k), part]
            rcopy(ref, ref, gs_send.at[a, k, i], gs_recv.at[a, k, i], sibling).wait_recv()

    n_sub = block // CHUNK

    def over(fn, blocks):
        for b in blocks:

            def sub(i, carry, b=b):
                fn(b, pl.ds(pl.multiple_of(i * CHUNK, CHUNK), CHUNK))
                return carry

            lax.fori_loop(0, n_sub, sub, 0)

    def over_all(fn):
        def one(i, carry):
            fn(i // n_sub, pl.ds(pl.multiple_of(lax.rem(i, n_sub) * CHUNK, CHUNK), CHUNK))
            return carry

        lax.fori_loop(0, n_resp * n_sub, one, 0)

    def score(b, rows):
        s = jnp.dot(kv[0, b, rows], q_t[...], preferred_element_type=F32) * scale
        st[b, rows] = s
        mx[...] = jnp.maximum(mx[...], fold(s, jnp.max))

    order = [k for k in (1, 3, 2) if k < n_y]
    gather_first(0)
    gather_first(1)
    over(score, [r])
    gather_sib(0, 0)
    over(score, [other(0)])
    for k in order:
        gather_y(0, k)
    for k in order:
        gather_z(0, k)
        over(score, [mine(k)])
    for k in order:
        gather_y(1, k)
    for k in order:
        gather_sib(0, k)
        over(score, [other(k)])

    mx[...] = jnp.broadcast_to(jnp.max(mx[...], axis=0, keepdims=True), mx.shape)
    m3 = mx[...][None]

    def expo(x):
        x3 = x.reshape(x.shape[0] // 8, 8, x.shape[1])
        return jnp.exp(x3 - mx[...][None]).reshape(x.shape)

    def times(x, v):
        return (x.reshape(x.shape[0] // 8, 8, x.shape[1]) * v[None]).reshape(x.shape)

    def minus(x, v):
        return (x.reshape(x.shape[0] // 8, 8, x.shape[1]) - v[None]).reshape(x.shape)

    e = expo(st_r[...])
    st_r[...] = e
    sm[...] = fold(e, jnp.sum)

    def soften(b, rows):
        e = expo(st[b, rows])
        st[b, rows] = e
        sm[...] += fold(e, jnp.sum)

    over_all(soften)
    sm[...] = jnp.broadcast_to(1.0 / jnp.sum(sm[...], axis=0, keepdims=True), sm.shape)
    for k in order:
        gather_z(1, k)

    def grad_out(a, b, rows, keep, value, yy):
        sel = rows.start // half
        if keep:
            acc[a, yy, sel] = value
        else:
            sib_send[a, yy, sel] = value.astype(BF16)

    def dv_chunk(yy, rows, keep):
        b = 2 * yy + (c if keep else 1 - c)
        p = times(st[b, rows], sm[...]).astype(BF16)
        pb[b, rows] = p
        grad_out(1, b, rows, keep, jnp.dot(p, do_s[...], preferred_element_type=F32), yy)

    def dk_chunk(yy, rows, keep):
        b = 2 * yy + (c if keep else 1 - c)
        ds = (times(st[b, rows], sm[...]) * minus(dp[b, rows], dl[...])).astype(BF16)
        pb[b, rows] = ds
        grad_out(0, b, rows, keep, jnp.dot(ds, q_s[...], preferred_element_type=F32) * scale, yy)

    def grad_pass(a, fn):
        for k in range(n_y - 1, -1, -1):
            yy = flip(y, k)
            over(lambda v, rows: fn(v, rows, False), [yy])
            start(
                rcopy(
                    sib_send.at[a, yy], sib_recv.at[a, yy], fs_send.at[a, k], fs_recv.at[a, k], sibling
                )
            )
        for k in range(n_y - 1, -1, -1):
            over(lambda v, rows: fn(v, rows, True), [flip(y, k)])

    def sum_sib(a):
        for k in range(n_y - 1, -1, -1):
            yy = flip(y, k)
            rcopy(
                sib_send.at[a, yy], sib_recv.at[a, yy], fs_send.at[a, k], fs_recv.at[a, k], sibling
            ).wait_recv()
            z_send[a, k] = (acc[a, yy, 1 - h] + sib_recv[a, yy, 1 - h].astype(F32)).astype(BF16)
            start(rcopy(z_send.at[a, k], z_recv.at[a, k], fz_send.at[a, k], fz_recv.at[a, k], zpair))
            acc[a, yy, h] += sib_recv[a, yy, h].astype(F32)

    def sum_z(a):
        for k in range(n_y - 1, -1, -1):
            yy = flip(y, k)
            rcopy(z_send.at[a, k], z_recv.at[a, k], fz_send.at[a, k], fz_recv.at[a, k], zpair).wait_recv()
            total = acc[a, yy, h] + z_recv[a, k].astype(F32)
            if k:
                y_send[a, k] = total.astype(BF16)
                start(rcopy(y_send.at[a, k], y_recv.at[a, k], fy_send.at[a, k], fy_recv.at[a, k], yline(k)))
            else:
                acc[a, yy, h] = total

    def sum_y(a):
        total = acc[a, y, h]
        for k in order:
            rcopy(y_send.at[a, k], y_recv.at[a, k], fy_send.at[a, k], fy_recv.at[a, k], yline(k)).wait_recv()
            total = total + y_recv[a, k].astype(F32)
        p_send[a] = total.astype(BF16)
        home = rcopy(p_send.at[a], p_recv.at[a], fp_send.at[a], fp_recv.at[a], owner)
        local = pltpu.make_async_copy(p_send.at[a], p_recv.at[a], fp_recv.at[a])

        @pl.when(away)
        def _():
            home.start()

        @pl.when(r == g)
        def _():
            local.start()

        return home

    p = times(st_r[...], sm[...]).astype(BF16)
    pb_r[...] = p
    rg_acc[1] = jnp.dot(p, do_s[...], preferred_element_type=F32)
    grad_pass(1, dv_chunk)
    sum_sib(1)

    d = jnp.dot(rkv[1], do_t[...], preferred_element_type=F32)
    dp_r[...] = d
    dl[...] = fold(pb_r[...].astype(F32) * d, jnp.sum)

    def dprob(b, rows):
        d = jnp.dot(kv[1, b, rows], do_t[...], preferred_element_type=F32)
        dp[b, rows] = d
        dl[...] += fold(pb[b, rows].astype(F32) * d, jnp.sum)

    over(dprob, [r])
    gather_sib(1, 0)
    over(dprob, [other(0)])
    for k in order:
        over(dprob, [mine(k)])
    for k in order:
        gather_sib(1, k)
        over(dprob, [other(k)])
    dl[...] = jnp.broadcast_to(jnp.sum(dl[...], axis=0, keepdims=True), dl.shape)
    sum_z(1)

    ds = (times(st_r[...], sm[...]) * minus(dp_r[...], dl[...])).astype(BF16)
    pb_r[...] = ds
    rg_acc[0] = jnp.dot(ds, q_s[...], preferred_element_type=F32) * scale
    own_rows = count // n_tp
    rg = jnp.concatenate(
        [rg_acc[0].reshape(n_tp, own_rows, HD), rg_acc[1].reshape(n_tp, own_rows, HD)], axis=1
    )
    rg_send[...] = rg.astype(BF16)

    def spread(d, carry):
        to = lax.rem(t + d, n_tp)
        rcopy(rg_send.at[to], rg_recv.at[t], rg_ssem.at[0], rg_rsem.at[0], {"resp": r, "tp": to}).start()
        return carry

    lax.fori_loop(1, n_tp, spread, 0)
    pltpu.make_async_copy(rg_send.at[t], rg_recv.at[t], rg_rsem.at[0]).start()

    grad_pass(0, dk_chunk)
    sum_sib(0)
    home_v = sum_y(1)

    def tdot(a, b):
        return lax.dot_general(a, b, (((0,), (0,)), ((), ())), preferred_element_type=F32)

    sum_z(0)

    def dq_block(b, total):
        return total + tdot(kv[0, b], pb[b])

    dq_t = lax.fori_loop(0, n_resp, dq_block, tdot(rkv[0], pb_r[...]))
    for j in range(heads):
        dq_ref[:, j * HD : (j + 1) * HD] = jnp.transpose(dq_t[:, j * count : (j + 1) * count]) * scale
    home_k = sum_y(0)

    pltpu.make_async_copy(rg_recv, rg_recv, rg_rsem.at[0]).wait()
    got = rg_recv[...].astype(F32)
    for i in range(n_tp // 2):
        both = got[2 * i] + got[2 * i + 1]
        rdk_ref[:, i * HD : (i + 1) * HD] = both[:own_rows]
        rdv_ref[:, i * HD : (i + 1) * HD] = both[own_rows:]

    home_v.wait_recv()
    pdv_ref[...] = p_recv[1].astype(F32)
    home_k.wait_recv()
    pdk_ref[...] = p_recv[0].astype(F32)

    for a in range(2):
        pltpu.make_async_copy(
            kv.at[a, 0, pl.ds(0, (n_tp - 1) * 16)], kv.at[a, 0, pl.ds(0, (n_tp - 1) * 16)], a_send.at[a]
        ).wait()
    pltpu.make_async_copy(
        rg_send.at[pl.ds(0, n_tp - 1)], rg_send.at[pl.ds(0, n_tp - 1)], rg_ssem.at[0]
    ).wait()
    for copy in sends:
        copy.wait_send()

    @pl.when(away)
    def _():
        home_v.wait_send()
        home_k.wait_send()


def solution(mesh):
    n_resp, n_tp = mesh.shape["resp"], mesh.shape["tp"]
    n_y = n_resp // 2

    def per_device(queries, resp_keys, resp_values, prefix_keys, prefix_values, cotangent, lengths):
        count, width = queries.shape
        heads = width // HD
        rows = heads * count
        block = n_tp * prefix_keys.shape[0]
        half = block // 2
        cols = prefix_keys.shape[1]
        dma = pltpu.SemaphoreType.DMA
        vmem = pltpu.VMEM
        any_spec = pl.BlockSpec(memory_space=pl.ANY)
        vmem_spec = pl.BlockSpec(memory_space=pltpu.VMEM)
        return pl.pallas_call(
            functools.partial(kernel, n_resp, n_tp),
            out_shape=(
                jax.ShapeDtypeStruct((count, width), F32),
                jax.ShapeDtypeStruct((count // n_tp, cols), F32),
                jax.ShapeDtypeStruct((count // n_tp, cols), F32),
                jax.ShapeDtypeStruct((half, HD), F32),
                jax.ShapeDtypeStruct((half, HD), F32),
            ),
            in_specs=[any_spec] * 6 + [pl.BlockSpec(memory_space=pltpu.SMEM)],
            out_specs=(vmem_spec,) * 5,
            scratch_shapes=[
                vmem((2, 16, cols), BF16),
                vmem((2, n_resp, block, HD), BF16),
                vmem((2, count, HD), BF16),
                vmem((rows, HD), BF16),
                vmem((rows, HD), BF16),
                vmem((HD, rows), BF16),
                vmem((HD, rows), BF16),
                vmem((n_resp, block, rows), F32),
                vmem((n_resp, block, rows), F32),
                vmem((n_resp, block, rows), BF16),
                vmem((count, rows), F32),
                vmem((count, rows), F32),
                vmem((count, rows), BF16),
                vmem((8, rows), F32),
                vmem((8, rows), F32),
                vmem((8, rows), F32),
                vmem((2, n_y, 2, half, HD), BF16),
                vmem((2, n_y, 2, half, HD), BF16),
                vmem((2, n_y, 2, half, HD), F32),
                vmem((2, n_y, half, HD), BF16),
                vmem((2, n_y, half, HD), BF16),
                vmem((2, n_y, half, HD), BF16),
                vmem((2, n_y, half, HD), BF16),
                vmem((2, half, HD), BF16),
                vmem((2, half, HD), BF16),
                vmem((n_tp, 16, HD), BF16),
                vmem((n_tp, 16, HD), BF16),
                vmem((2, count, HD), F32),
                dma((4 + 2 * heads,)),
                dma((2,)),
                dma((2,)),
                dma((2, n_y)),
                dma((2, n_y)),
                dma((2, n_y)),
                dma((2, n_y)),
                dma((2, n_y, 2)),
                dma((2, n_y, 2)),
                dma((2, n_y)),
                dma((2, n_y)),
                dma((2, n_y)),
                dma((2, n_y)),
                dma((2, n_y)),
                dma((2, n_y)),
                dma((2,)),
                dma((2,)),
                dma((1,)),
                dma((1,)),
            ],
            compiler_params=pltpu.CompilerParams(
                collective_id=0, has_side_effects=True, vmem_limit_bytes=48 * 1024 * 1024
            ),
            cost_estimate=pl.CostEstimate(
                flops=10 * rows * (n_resp * block + count) * HD,
                bytes_accessed=4 * 1024 * 1024,
                transcendentals=rows * (n_resp * block + count),
            ),
        )(queries, resp_keys, resp_values, prefix_keys, prefix_values, cotangent, lengths)

    return jax.shard_map(
        per_device,
        mesh=mesh,
        in_specs=(
            P(("grp", "resp"), "tp"),
            P(("grp", "resp"), None),
            P(("grp", "resp"), None),
            P(("grp", "resp", "tp"), None),
            P(("grp", "resp", "tp"), None),
            P(("grp", "resp"), "tp"),
            P("grp"),
        ),
        out_specs=(
            P(("grp", "resp"), "tp"),
            P(("grp", "resp", "tp"), None),
            P(("grp", "resp", "tp"), None),
            P(("grp", "tp"), "resp"),
            P(("grp", "tp"), "resp"),
        ),
        check_vma=False,
    )
```

time: 909 us -> 70.1 us (0.08)
  the two profiles are of different devices: /device:TPU:1 before, /device:TPU:26 now
where the time goes in v1:
time: 70.1 us; the launch traced here: 69.8 us
  Pallas kernels  60 us (86%)
  local copies, waits for them, and re-layouts  9.06 us (13%)
    pallas_call x1, Pallas kernels, per_device(): pl.pallas_call(functools.partial(kernel, n_resp, n_tp), out_shape=(jax.Sh...  60 us
    unnamed x19, local copies, waits for them, and re-layouts  9.06 us

profile of v1, /device:TPU:26, one launch (start us, length us, event | category | flops | bytes accessed | tf_op | source)
XLA Modules:
  0.0 69.8 jit_solution(9457813033250729451)
XLA Ops:
  0.6 0.0 copy-start
  0.6 0.9 %copy-done = bf16[128,1024]{1,0:T(8,128)(2,1)S(1)} copy-done((bf16[128,1024]{1,0:T(8,128)(2,1)S(1)}, bf16[128,1024]{1,0:T(8,128)(2,1)}, u32[]{:S(2)}) %copy-start) | copy-done | bytes 262168
  1.6 0.0 copy-start.1
  1.6 0.9 %copy-done.1 = bf16[128,1024]{1,0:T(8,128)(2,1)S(1)} copy-done((bf16[128,1024]{1,0:T(8,128)(2,1)S(1)}, bf16[128,1024]{1,0:T(8,128)(2,1)}, u32[]{:S(2)}) %copy-start.1) | copy-done | bytes 262168
  2.5 0.0 copy-start.2
  2.5 0.9 %copy-done.2 = bf16[128,512]{1,0:T(8,128)(2,1)S(1)} copy-done((bf16[128,512]{1,0:T(8,128)(2,1)S(1)}, bf16[128,512]{1,0:T(8,128)(2,1)}, u32[]{:S(2)}) %copy-start.2) | copy-done | bytes 131096
  3.4 0.0 copy-start.3
  3.4 0.9 %copy-done.3 = bf16[128,512]{1,0:T(8,128)(2,1)S(1)} copy-done((bf16[128,512]{1,0:T(8,128)(2,1)S(1)}, bf16[128,512]{1,0:T(8,128)(2,1)}, u32[]{:S(2)}) %copy-start.3) | copy-done | bytes 131096
  4.3 0.0 copy-start.4
  4.3 0.8 %copy-done.4 = bf16[16,1024]{1,0:T(8,128)(2,1)S(1)} copy-done((bf16[16,1024]{1,0:T(8,128)(2,1)S(1)}, bf16[16,1024]{1,0:T(8,128)(2,1)}, u32[]{:S(2)}) %copy-start.4) | copy-done | bytes 32792
  5.1 0.0 copy-start.5
  5.1 0.8 %copy-done.5 = bf16[16,1024]{1,0:T(8,128)(2,1)S(1)} copy-done((bf16[16,1024]{1,0:T(8,128)(2,1)S(1)}, bf16[16,1024]{1,0:T(8,128)(2,1)}, u32[]{:S(2)}) %copy-start.5) | copy-done | bytes 32792
  5.9 0.0 copy-start.6
  5.9 0.7 copy-done.6
  6.5 60.0 %shard_map.110 = (f32[128,512]{1,0:T(8,128)S(1)}, f32[8,1024]{1,0:T(8,128)S(1)}, f32[8,1024]{1,0:T(8,128)S(1)}, f32[128,128]{1,0:T(8,128)S(1)}, f32[128,128]{1,0:T(8,128)S(1)}) custom-call(bf16[128,512]{1,0:T(8,128)(2,1)S(1)} %copy-done.2, bf16[128,1024]{1,0:T(8,128)(2,1)S(1)} %copy-done, bf16[128,1024]{1,0:T(8,128)(2,1)S(1)} %copy-done.1, ...), custom_call_target="tpu_custom_call" | custom-call | flops 1426063360 | bytes 4194304 | tf_op jit(solution)/shard_map/pallas_call | solution.py:470
  66.6 0.7 %copy.17 = f32[128,512]{1,0:T(8,128)} copy(f32[128,512]{1,0:T(8,128)S(1)} %get-tuple-element.10) | data formatting | bytes 524288
  67.3 0.6 copy.18
  67.9 0.6 copy.19
  68.5 0.6 copy.20
  69.1 0.6 copy.21
Async XLA Ops:
  0.6 1.0 %copy-start = (bf16[128,1024]{1,0:T(8,128)(2,1)S(1)}, bf16[128,1024]{1,0:T(8,128)(2,1)}, u32[]{:S(2)}) copy-start(bf16[128,1024]{1,0:T(8,128)(2,1)} %rk_hbm.1) | copy-start | bytes 786436
  1.6 0.9 %copy-start.1 = (bf16[128,1024]{1,0:T(8,128)(2,1)S(1)}, bf16[128,1024]{1,0:T(8,128)(2,1)}, u32[]{:S(2)}) copy-start(bf16[128,1024]{1,0:T(8,128)(2,1)} %rv_hbm.1) | copy-start | bytes 786436
  2.5 0.9 %copy-start.2 = (bf16[128,512]{1,0:T(8,128)(2,1)S(1)}, bf16[128,512]{1,0:T(8,128)(2,1)}, u32[]{:S(2)}) copy-start(bf16[128,512]{1,0:T(8,128)(2,1)} %q_hbm.1) | copy-start | bytes 393220
  3.4 0.9 %copy-start.3 = (bf16[128,512]{1,0:T(8,128)(2,1)S(1)}, bf16[128,512]{1,0:T(8,128)(2,1)}, u32[]{:S(2)}) copy-start(bf16[128,512]{1,0:T(8,128)(2,1)} %ct_hbm.1) | copy-start | bytes 393220
  4.3 0.8 %copy-start.4 = (bf16[16,1024]{1,0:T(8,128)(2,1)S(1)}, bf16[16,1024]{1,0:T(8,128)(2,1)}, u32[]{:S(2)}) copy-start(bf16[16,1024]{1,0:T(8,128)(2,1)} %pk_hbm.1) | copy-start | bytes 98308
  5.1 0.8 %copy-start.5 = (bf16[16,1024]{1,0:T(8,128)(2,1)S(1)}, bf16[16,1024]{1,0:T(8,128)(2,1)}, u32[]{:S(2)}) copy-start(bf16[16,1024]{1,0:T(8,128)(2,1)} %pv_hbm.1) | copy-start | bytes 98308
  5.9 0.7 copy-start.6

commit v2 on v1

--- a/solution.py
+++ b/solution.py
@@ -70,13 +70,10 @@
     rg_send,
     rg_recv,
     rg_acc,
+    sent,
     in_sem,
     a_send,
     a_recv,
-    gy_send,
-    gy_recv,
-    gz_send,
-    gz_recv,
     gs_send,
     gs_recv,
     fs_send,
@@ -131,42 +128,48 @@
     for load in loads:
         load.start()
 
+    n_z = n_tp // 2
+    n_ring = 2 * n_y
+    y_all, z = lax.rem(t, n_tp) // n_z * n_y + y, lax.rem(t, n_z)
+    ys = [lax.rem(y_all + d, n_ring) for d in range(n_ring)]
+    zs = [lax.rem(z + d, n_z) for d in range(n_z)]
+    resp_of = [2 * lax.rem(v, n_y) + c for v in ys]
+    tp_of = [v // n_y * n_z for v in ys]
+
+    def hops(d, n):
+        return min(d, n - d)
+
+    offsets = [(i, j) for i in range(n_ring) for j in range(n_z) if i or j]
+    offsets.sort(key=lambda o: -hops(o[0], n_ring) - hops(o[1], n_z))
+
     barrier = pltpu.get_barrier_semaphore()
-
-    def greet(d, carry):
+    for i, j in offsets:
         pl.semaphore_signal(
-            barrier, inc=1, device_id={"resp": r, "tp": lax.rem(t + d, n_tp)}, device_id_type=MESH
+            barrier, inc=1, device_id={"resp": resp_of[i], "tp": tp_of[i] + zs[j]}, device_id_type=MESH
         )
-        return carry
-
-    lax.fori_loop(1, n_tp, greet, 0)
     pl.semaphore_signal(barrier, inc=1, device_id=sibling, device_id_type=MESH)
-    for k in range(1, n_y):
-        pl.semaphore_signal(barrier, inc=1, device_id=yline(k), device_id_type=MESH)
 
     @pl.when(away)
     def _():
         pl.semaphore_signal(barrier, inc=1, device_id=owner, device_id_type=MESH)
 
-    pl.semaphore_wait(barrier, n_tp - 1 + n_y + away.astype(jnp.int32))
-
-    rows16 = pl.ds(pl.multiple_of(t * 16, 16), 16)
     for a in range(2):
         loads[a].wait()
-
-        def scatter(d, carry, a=a):
-            to = lax.rem(t + d, n_tp)
+    pl.semaphore_wait(barrier, len(offsets) + 1 + away.astype(jnp.int32))
+
+    rows16 = pl.ds(pl.multiple_of(t * 16, 16), 16)
+    spot = c * n_y + y
+    for a in range(2):
+        for i, j in offsets:
+            to = tp_of[i] + zs[j]
             rcopy(
-                pin.at[a, :, pl.ds(pl.multiple_of((to // 2) * HD, HD), HD)],
-                kv.at[a, r, rows16],
+                pin.at[a, :, pl.ds(pl.multiple_of(to // 2 * HD, HD), HD)],
+                kv.at[a, spot, rows16],
                 a_send.at[a],
                 a_recv.at[a],
-                {"resp": r, "tp": to},
+                {"resp": resp_of[i], "tp": to},
             ).start()
-            return carry
-
-        lax.fori_loop(1, n_tp, scatter, 0)
-        pltpu.make_async_copy(pin.at[a, :, pl.ds(col, HD)], kv.at[a, r, rows16], a_recv.at[a]).start()
+        pltpu.make_async_copy(pin.at[a, :, pl.ds(col, HD)], kv.at[a, spot, rows16], a_recv.at[a]).start()
 
     for load in loads[2:]:
         load.wait()
@@ -184,65 +187,30 @@
     st_r[...] = s
     mx[...] = fold(s, jnp.max)
 
-    def mine(k):
-        return 2 * flip(y, k) + c
-
-    def other(k):
-        return 2 * flip(y, k) + 1 - c
-
-    own_half = pl.ds(pl.multiple_of(h * half, half), half)
-    far_half = pl.ds(pl.multiple_of((1 - h) * half, half), half)
-
     sends = []
 
     def start(copy):
         copy.start()
         sends.append(copy)
 
-    def gather_first(a):
-        pltpu.make_async_copy(kv.at[a, r], kv.at[a, r], a_recv.at[a]).wait()
-        for k in range(n_y - 1, 0, -1):
-            ref = kv.at[a, r, own_half]
-            start(rcopy(ref, ref, gy_send.at[a, k], gy_recv.at[a, k], yline(k)))
-        start(rcopy(kv.at[a, r], kv.at[a, r], gs_send.at[a, 0, 0], gs_recv.at[a, 0, 0], sibling))
-
-    def gather_y(a, k):
-        ref = kv.at[a, mine(k), own_half]
-        rcopy(ref, ref, gy_send.at[a, k], gy_recv.at[a, k], yline(k)).wait_recv()
-        start(rcopy(ref, ref, gz_send.at[a, k], gz_recv.at[a, k], zpair))
-        start(rcopy(ref, ref, gs_send.at[a, k, 0], gs_recv.at[a, k, 0], sibling))
-
-    def gather_z(a, k):
-        ref = kv.at[a, mine(k), far_half]
-        rcopy(ref, ref, gz_send.at[a, k], gz_recv.at[a, k], zpair).wait_recv()
-        start(rcopy(ref, ref, gs_send.at[a, k, 1], gs_recv.at[a, k, 1], sibling))
-
-    def gather_sib(a, k):
-        if k == 0:
-            ref = kv.at[a, other(0)]
-            rcopy(ref, ref, gs_send.at[a, 0, 0], gs_recv.at[a, 0, 0], sibling).wait_recv()
-            return
-        for i, part in enumerate((own_half, far_half)):
-            ref = kv.at[a, other(k), part]
-            rcopy(ref, ref, gs_send.at[a, k, i], gs_recv.at[a, k, i], sibling).wait_recv()
+    near = pl.ds(c * n_y, n_y)
+    far = pl.ds((1 - c) * n_y, n_y)
+
+    def gather(a):
+        pltpu.make_async_copy(kv.at[a, near], kv.at[a, near], a_recv.at[a]).wait()
+        start(rcopy(kv.at[a, near], kv.at[a, near], gs_send.at[a], gs_recv.at[a], sibling))
+
+    def gather_sib(a):
+        rcopy(kv.at[a, far], kv.at[a, far], gs_send.at[a], gs_recv.at[a], sibling).wait_recv()
 
     n_sub = block // CHUNK
 
-    def over(fn, blocks):
-        for b in blocks:
-
-            def sub(i, carry, b=b):
-                fn(b, pl.ds(pl.multiple_of(i * CHUNK, CHUNK), CHUNK))
-                return carry
-
-            lax.fori_loop(0, n_sub, sub, 0)
-
-    def over_all(fn):
+    def over(fn, first, blocks):
         def one(i, carry):
-            fn(i // n_sub, pl.ds(pl.multiple_of(lax.rem(i, n_sub) * CHUNK, CHUNK), CHUNK))
+            fn(first + i // n_sub, pl.ds(pl.multiple_of(lax.rem(i, n_sub) * CHUNK, CHUNK), CHUNK))
             return carry
 
-        lax.fori_loop(0, n_resp * n_sub, one, 0)
+        lax.fori_loop(0, blocks * n_sub, one, 0)
 
     def score(b, rows):
         s = jnp.dot(kv[0, b, rows], q_t[...], preferred_element_type=F32) * scale
@@ -250,21 +218,10 @@
         mx[...] = jnp.maximum(mx[...], fold(s, jnp.max))
 
     order = [k for k in (1, 3, 2) if k < n_y]
-    gather_first(0)
-    gather_first(1)
-    over(score, [r])
-    gather_sib(0, 0)
-    over(score, [other(0)])
-    for k in order:
-        gather_y(0, k)
-    for k in order:
-        gather_z(0, k)
-        over(score, [mine(k)])
-    for k in order:
-        gather_y(1, k)
-    for k in order:
-        gather_sib(0, k)
-        over(score, [other(k)])
+    gather(0)
+    over(score, c * n_y, n_y)
+    gather_sib(0)
+    over(score, (1 - c) * n_y, n_y)
 
     mx[...] = jnp.broadcast_to(jnp.max(mx[...], axis=0, keepdims=True), mx.shape)
     m3 = mx[...][None]
@@ -288,10 +245,8 @@
         st[b, rows] = e
         sm[...] += fold(e, jnp.sum)
 
-    over_all(soften)
+    over(soften, 0, n_resp)
     sm[...] = jnp.broadcast_to(1.0 / jnp.sum(sm[...], axis=0, keepdims=True), sm.shape)
-    for k in order:
-        gather_z(1, k)
 
     def grad_out(a, b, rows, keep, value, yy):
         sel = rows.start // half
@@ -300,33 +255,28 @@
         else:
             sib_send[a, yy, sel] = value.astype(BF16)
 
-    def dv_chunk(yy, rows, keep):
-        b = 2 * yy + (c if keep else 1 - c)
+    def dv_chunk(b, rows, keep):
         p = times(st[b, rows], sm[...]).astype(BF16)
         pb[b, rows] = p
-        grad_out(1, b, rows, keep, jnp.dot(p, do_s[...], preferred_element_type=F32), yy)
-
-    def dk_chunk(yy, rows, keep):
-        b = 2 * yy + (c if keep else 1 - c)
+        grad_out(1, b, rows, keep, jnp.dot(p, do_s[...], preferred_element_type=F32), lax.rem(b, n_y))
+
+    def dk_chunk(b, rows, keep):
         ds = (times(st[b, rows], sm[...]) * minus(dp[b, rows], dl[...])).astype(BF16)
         pb[b, rows] = ds
-        grad_out(0, b, rows, keep, jnp.dot(ds, q_s[...], preferred_element_type=F32) * scale, yy)
+        grad_out(0, b, rows, keep, jnp.dot(ds, q_s[...], preferred_element_type=F32) * scale, lax.rem(b, n_y))
 
     def grad_pass(a, fn):
         for k in range(n_y - 1, -1, -1):
             yy = flip(y, k)
-            over(lambda v, rows: fn(v, rows, False), [yy])
+            over(lambda b, rows: fn(b, rows, False), (1 - c) * n_y + yy, 1)
             start(
                 rcopy(
                     sib_send.at[a, yy], sib_recv.at[a, yy], fs_send.at[a, k], fs_recv.at[a, k], sibling
                 )
             )
         for k in range(n_y - 1, -1, -1):
-            over(lambda v, rows: fn(v, rows, True), [flip(y, k)])
-
-    def sum_sib(a):
-        for k in range(n_y - 1, -1, -1):
             yy = flip(y, k)
+            over(lambda b, rows: fn(b, rows, True), c * n_y + yy, 1)
             rcopy(
                 sib_send.at[a, yy], sib_recv.at[a, yy], fs_send.at[a, k], fs_recv.at[a, k], sibling
             ).wait_recv()
@@ -368,7 +318,7 @@
     pb_r[...] = p
     rg_acc[1] = jnp.dot(p, do_s[...], preferred_element_type=F32)
     grad_pass(1, dv_chunk)
-    sum_sib(1)
+    gather(1)
 
     d = jnp.dot(rkv[1], do_t[...], preferred_element_type=F32)
     dp_r[...] = d
@@ -379,16 +329,11 @@
         dp[b, rows] = d
         dl[...] += fold(pb[b, rows].astype(F32) * d, jnp.sum)
 
-    over(dprob, [r])
-    gather_sib(1, 0)
-    over(dprob, [other(0)])
-    for k in order:
-        over(dprob, [mine(k)])
-    for k in order:
-        gather_sib(1, k)
-        over(dprob, [other(k)])
+    over(dprob, c * n_y, n_y)
+    sum_z(1)
+    gather_sib(1)
+    over(dprob, (1 - c) * n_y, n_y)
     dl[...] = jnp.broadcast_to(jnp.sum(dl[...], axis=0, keepdims=True), dl.shape)
-    sum_z(1)
 
     ds = (times(st_r[...], sm[...]) * minus(dp_r[...], dl[...])).astype(BF16)
     pb_r[...] = ds
@@ -408,13 +353,10 @@
     pltpu.make_async_copy(rg_send.at[t], rg_recv.at[t], rg_rsem.at[0]).start()
 
     grad_pass(0, dk_chunk)
-    sum_sib(0)
     home_v = sum_y(1)
 
     def tdot(a, b):
         return lax.dot_general(a, b, (((0,), (0,)), ((), ())), preferred_element_type=F32)
-
-    sum_z(0)
 
     def dq_block(b, total):
         return total + tdot(kv[0, b], pb[b])
@@ -422,7 +364,7 @@
     dq_t = lax.fori_loop(0, n_resp, dq_block, tdot(rkv[0], pb_r[...]))
     for j in range(heads):
         dq_ref[:, j * HD : (j + 1) * HD] = jnp.transpose(dq_t[:, j * count : (j + 1) * count]) * scale
-    home_k = sum_y(0)
+    sum_z(0)
 
     pltpu.make_async_copy(rg_recv, rg_recv, rg_rsem.at[0]).wait()
     got = rg_recv[...].astype(F32)
@@ -431,6 +373,7 @@
         rdk_ref[:, i * HD : (i + 1) * HD] = both[:own_rows]
         rdv_ref[:, i * HD : (i + 1) * HD] = both[own_rows:]
 
+    home_k = sum_y(0)
     home_v.wait_recv()
     pdv_ref[...] = p_recv[1].astype(F32)
     home_k.wait_recv()
@@ -438,7 +381,7 @@
 
     for a in range(2):
         pltpu.make_async_copy(
-            kv.at[a, 0, pl.ds(0, (n_tp - 1) * 16)], kv.at[a, 0, pl.ds(0, (n_tp - 1) * 16)], a_send.at[a]
+            sent.at[pl.ds(0, len(offsets))], sent.at[pl.ds(0, len(offsets))], a_send.at[a]
         ).wait()
     pltpu.make_async_copy(
         rg_send.at[pl.ds(0, n_tp - 1)], rg_send.at[pl.ds(0, n_tp - 1)], rg_ssem.at[0]
@@ -507,15 +450,12 @@
                 vmem((n_tp, 16, HD), BF16),
                 vmem((n_tp, 16, HD), BF16),
                 vmem((2, count, HD), F32),
+                vmem((n_resp * n_tp // 2, 16, HD), BF16),
                 dma((4 + 2 * heads,)),
                 dma((2,)),
                 dma((2,)),
-                dma((2, n_y)),
-                dma((2, n_y)),
-                dma((2, n_y)),
-                dma((2, n_y)),
-                dma((2, n_y, 2)),
-                dma((2, n_y, 2)),
+                dma((2,)),
+                dma((2,)),
                 dma((2, n_y)),
                 dma((2, n_y)),
                 dma((2, n_y)),
@@ -528,7 +468,7 @@
                 dma((1,)),
             ],
             compiler_params=pltpu.CompilerParams(
-                collective_id=0, has_side_effects=True, vmem_limit_bytes=48 * 1024 * 1024
+                collective_id=0, has_side_effects=True, vmem_limit_bytes=62 * 1024 * 1024
             ),
             cost_estimate=pl.CostEstimate(
                 flops=10 * rows * (n_resp * block + count) * HD,

time: 70.1 us -> 62.6 us (0.89)
  the two profiles are of different devices: /device:TPU:26 before, /device:TPU:44 now
where the time goes in v2:
time: 62.6 us; the launch traced here: 62.4 us
  Pallas kernels  57.3 us (92%)
  local copies, waits for them, and re-layouts  4.41 us (7%)
  between operations  0.66 us (1%)
    pallas_call x1, Pallas kernels, per_device(): pl.pallas_call(functools.partial(kernel, n_resp, n_tp), out_shape=(jax.Sh...  57.3 us
    unnamed x13, local copies, waits for them, and re-layouts  4.41 us

profile of v2, /device:TPU:44, one launch (start us, length us, event | category | flops | bytes accessed | tf_op | source)
XLA Modules:
  0.0 62.4 jit_solution(10927727254231805488)
XLA Ops:
  0.6 57.3 %shard_map.110 = (f32[128,512]{1,0:T(8,128)}, f32[8,1024]{1,0:T(8,128)}, f32[8,1024]{1,0:T(8,128)}, f32[128,128]{1,0:T(8,128)}, f32[128,128]{1,0:T(8,128)}) custom-call(bf16[128,512]{1,0:T(8,128)(2,1)} %q_hbm.1, bf16[128,1024]{1,0:T(8,128)(2,1)} %rk_hbm.1, bf16[128,1024]{1,0:T(8,128)(2,1)} %rv_hbm.1, bf16[16,1024]{1,0:T(8,128)(2,1)} %pk_hbm.1, ...), custom_call_target="tpu_custom_call" | custom-call | flops 1426063360 | bytes 4194304 | tf_op jit(solution)/shard_map/pallas_call | solution.py:413
  57.9 0.0 copy-start.3
  57.9 0.0 copy-start.2
  58.0 1.7 %copy.17 = f32[128,512]{1,0:T(8,128)} copy(f32[128,512]{1,0:T(8,128)} %get-tuple-element.10) | data formatting | bytes 524288
  59.6 0.0 copy-done.3
  59.6 0.0 copy-start.1
  59.6 0.6 copy.18
  60.3 0.0 copy-done.2
  60.3 0.6 copy.19
  60.9 0.0 copy-done.1
  60.9 0.0 copy-start
  60.9 0.6 %copy.20 = f32[128,128]{1,0:T(8,128)} copy(f32[128,128]{1,0:T(8,128)S(1)} %copy-done.1) | data formatting | bytes 131072
  61.5 0.2 copy-done
  61.7 0.6 %copy.21 = f32[128,128]{1,0:T(8,128)} copy(f32[128,128]{1,0:T(8,128)S(1)} %copy-done) | data formatting | bytes 131072
Async XLA Ops:
  57.9 1.7 %copy-start.3 = (f32[8,1024]{1,0:T(8,128)S(1)}, f32[8,1024]{1,0:T(8,128)}, u32[]{:S(2)}) copy-start(f32[8,1024]{1,0:T(8,128)} %get-tuple-element.11) | copy-start | bytes 98308
  57.9 2.3 %copy-start.2 = (f32[8,1024]{1,0:T(8,128)S(1)}, f32[8,1024]{1,0:T(8,128)}, u32[]{:S(2)}) copy-start(f32[8,1024]{1,0:T(8,128)} %get-tuple-element.12) | copy-start | bytes 98308
  59.6 1.2 %copy-start.1 = (f32[128,128]{1,0:T(8,128)S(1)}, f32[128,128]{1,0:T(8,128)}, u32[]{:S(2)}) copy-start(f32[128,128]{1,0:T(8,128)} %get-tuple-element.13) | copy-start | bytes 196612
  60.9 0.9 %copy-start = (f32[128,128]{1,0:T(8,128)S(1)}, f32[128,128]{1,0:T(8,128)}, u32[]{:S(2)}) copy-start(f32[128,128]{1,0:T(8,128)} %get-tuple-element.14) | copy-start | bytes 196612

commit v3 on v2

--- a/solution.py
+++ b/solution.py
@@ -10,7 +10,7 @@
 
 MESH = pl.DeviceIdType.MESH
 HD = 128
-CHUNK = 128
+UNROLL = 4
 F32 = jnp.float32
 BF16 = jnp.bfloat16
 
@@ -203,18 +203,12 @@
     def gather_sib(a):
         rcopy(kv.at[a, far], kv.at[a, far], gs_send.at[a], gs_recv.at[a], sibling).wait_recv()
 
-    n_sub = block // CHUNK
-
     def over(fn, first, blocks):
-        def one(i, carry):
-            fn(first + i // n_sub, pl.ds(pl.multiple_of(lax.rem(i, n_sub) * CHUNK, CHUNK), CHUNK))
-            return carry
-
-        lax.fori_loop(0, blocks * n_sub, one, 0)
-
-    def score(b, rows):
-        s = jnp.dot(kv[0, b, rows], q_t[...], preferred_element_type=F32) * scale
-        st[b, rows] = s
+        lax.fori_loop(0, blocks, lambda i, carry: fn(first + i), None, unroll=UNROLL)
+
+    def score(b):
+        s = jnp.dot(kv[0, b], q_t[...], preferred_element_type=F32) * scale
+        st[b] = s
         mx[...] = jnp.maximum(mx[...], fold(s, jnp.max))
 
     order = [k for k in (1, 3, 2) if k < n_y]
@@ -224,8 +218,6 @@
     over(score, (1 - c) * n_y, n_y)
 
     mx[...] = jnp.broadcast_to(jnp.max(mx[...], axis=0, keepdims=True), mx.shape)
-    m3 = mx[...][None]
-
     def expo(x):
         x3 = x.reshape(x.shape[0] // 8, 8, x.shape[1])
         return jnp.exp(x3 - mx[...][None]).reshape(x.shape)
@@ -240,35 +232,35 @@
     st_r[...] = e
     sm[...] = fold(e, jnp.sum)
 
-    def soften(b, rows):
-        e = expo(st[b, rows])
-        st[b, rows] = e
+    def soften(b):
+        e = expo(st[b])
+        st[b] = e
         sm[...] += fold(e, jnp.sum)
 
     over(soften, 0, n_resp)
     sm[...] = jnp.broadcast_to(1.0 / jnp.sum(sm[...], axis=0, keepdims=True), sm.shape)
 
-    def grad_out(a, b, rows, keep, value, yy):
-        sel = rows.start // half
+    def grad_out(a, b, keep, value):
+        value = value.reshape(2, half, HD)
         if keep:
-            acc[a, yy, sel] = value
+            acc[a, lax.rem(b, n_y)] = value
         else:
-            sib_send[a, yy, sel] = value.astype(BF16)
-
-    def dv_chunk(b, rows, keep):
-        p = times(st[b, rows], sm[...]).astype(BF16)
-        pb[b, rows] = p
-        grad_out(1, b, rows, keep, jnp.dot(p, do_s[...], preferred_element_type=F32), lax.rem(b, n_y))
-
-    def dk_chunk(b, rows, keep):
-        ds = (times(st[b, rows], sm[...]) * minus(dp[b, rows], dl[...])).astype(BF16)
-        pb[b, rows] = ds
-        grad_out(0, b, rows, keep, jnp.dot(ds, q_s[...], preferred_element_type=F32) * scale, lax.rem(b, n_y))
+            sib_send[a, lax.rem(b, n_y)] = value.astype(BF16)
+
+    def dv_block(b, keep):
+        p = times(st[b], sm[...]).astype(BF16)
+        pb[b] = p
+        grad_out(1, b, keep, jnp.dot(p, do_s[...], preferred_element_type=F32))
+
+    def dk_block(b, keep):
+        ds = (times(st[b], sm[...]) * minus(dp[b], dl[...])).astype(BF16)
+        pb[b] = ds
+        grad_out(0, b, keep, jnp.dot(ds, q_s[...], preferred_element_type=F32) * scale)
 
     def grad_pass(a, fn):
         for k in range(n_y - 1, -1, -1):
             yy = flip(y, k)
-            over(lambda b, rows: fn(b, rows, False), (1 - c) * n_y + yy, 1)
+            fn((1 - c) * n_y + yy, False)
             start(
                 rcopy(
                     sib_send.at[a, yy], sib_recv.at[a, yy], fs_send.at[a, k], fs_recv.at[a, k], sibling
@@ -276,7 +268,7 @@
             )
         for k in range(n_y - 1, -1, -1):
             yy = flip(y, k)
-            over(lambda b, rows: fn(b, rows, True), c * n_y + yy, 1)
+            fn(c * n_y + yy, True)
             rcopy(
                 sib_send.at[a, yy], sib_recv.at[a, yy], fs_send.at[a, k], fs_recv.at[a, k], sibling
             ).wait_recv()
@@ -317,17 +309,17 @@
     p = times(st_r[...], sm[...]).astype(BF16)
     pb_r[...] = p
     rg_acc[1] = jnp.dot(p, do_s[...], preferred_element_type=F32)
-    grad_pass(1, dv_chunk)
+    grad_pass(1, dv_block)
     gather(1)
 
     d = jnp.dot(rkv[1], do_t[...], preferred_element_type=F32)
     dp_r[...] = d
     dl[...] = fold(pb_r[...].astype(F32) * d, jnp.sum)
 
-    def dprob(b, rows):
-        d = jnp.dot(kv[1, b, rows], do_t[...], preferred_element_type=F32)
-        dp[b, rows] = d
-        dl[...] += fold(pb[b, rows].astype(F32) * d, jnp.sum)
+    def dprob(b):
+        d = jnp.dot(kv[1, b], do_t[...], preferred_element_type=F32)
+        dp[b] = d
+        dl[...] += fold(pb[b].astype(F32) * d, jnp.sum)
 
     over(dprob, c * n_y, n_y)
     sum_z(1)
@@ -352,16 +344,13 @@
     lax.fori_loop(1, n_tp, spread, 0)
     pltpu.make_async_copy(rg_send.at[t], rg_recv.at[t], rg_rsem.at[0]).start()
 
-    grad_pass(0, dk_chunk)
+    grad_pass(0, dk_block)
     home_v = sum_y(1)
 
     def tdot(a, b):
         return lax.dot_general(a, b, (((0,), (0,)), ((), ())), preferred_element_type=F32)
 
-    def dq_block(b, total):
-        return total + tdot(kv[0, b], pb[b])
-
-    dq_t = lax.fori_loop(0, n_resp, dq_block, tdot(rkv[0], pb_r[...]))
+    dq_t = tdot(rkv[0], pb_r[...]) + tdot(kv[0].reshape(n_resp * block, HD), pb[...].reshape(n_resp * block, heads * count))
     for j in range(heads):
         dq_ref[:, j * HD : (j + 1) * HD] = jnp.transpose(dq_t[:, j * count : (j + 1) * count]) * scale
     sum_z(0)
@@ -393,6 +382,15 @@
     def _():
         home_v.wait_send()
         home_k.wait_send()
+
+
+def write_out(*refs):
+    sem = refs[10]
+    copies = [pltpu.make_async_copy(refs[i], refs[5 + i], sem.at[i]) for i in range(5)]
+    for copy in copies:
+        copy.start()
+    for copy in copies:
+        copy.wait()
 
 
 def solution(mesh):
@@ -410,15 +408,10 @@
         vmem = pltpu.VMEM
         any_spec = pl.BlockSpec(memory_space=pl.ANY)
         vmem_spec = pl.BlockSpec(memory_space=pltpu.VMEM)
-        return pl.pallas_call(
+        shapes = ((count, width), (count // n_tp, cols), (count // n_tp, cols), (half, HD), (half, HD))
+        results = pl.pallas_call(
             functools.partial(kernel, n_resp, n_tp),
-            out_shape=(
-                jax.ShapeDtypeStruct((count, width), F32),
-                jax.ShapeDtypeStruct((count // n_tp, cols), F32),
-                jax.ShapeDtypeStruct((count // n_tp, cols), F32),
-                jax.ShapeDtypeStruct((half, HD), F32),
-                jax.ShapeDtypeStruct((half, HD), F32),
-            ),
+            out_shape=tuple(pltpu.VMEM(shape, F32) for shape in shapes),
             in_specs=[any_spec] * 6 + [pl.BlockSpec(memory_space=pltpu.SMEM)],
             out_specs=(vmem_spec,) * 5,
             scratch_shapes=[
@@ -476,6 +469,13 @@
                 transcendentals=rows * (n_resp * block + count),
             ),
         )(queries, resp_keys, resp_values, prefix_keys, prefix_values, cotangent, lengths)
+        return pl.pallas_call(
+            write_out,
+            out_shape=tuple(jax.ShapeDtypeStruct(shape, F32) for shape in shapes),
+            in_specs=[any_spec] * 5,
+            out_specs=(any_spec,) * 5,
+            scratch_shapes=[dma((5,))],
+        )(*results)
 
     return jax.shard_map(
         per_device,

time: 62.6 us -> 71.7 us (1.15)
  the two profiles are of different devices: /device:TPU:44 before, /device:TPU:46 now
where the time goes in v3:
time: 71.7 us; the launch traced here: 71.5 us
  Pallas kernels  67.7 us (94%)
  local copies, waits for them, and re-layouts  3.13 us (4%)
    pallas_call x1, Pallas kernels, per_device(): pl.pallas_call(functools.partial(kernel, n_resp, n_tp), out_shape=tuple((...  52.7 us
    pallas_call x1, Pallas kernels, per_device(): pl.pallas_call(write_out, out_shape=tuple((jax.ShapeDtypeStruct(shape, F3...  15 us
    unnamed x10, local copies, waits for them, and re-layouts  3.13 us

profile of v3, /device:TPU:46, one launch (start us, length us, event | category | flops | bytes accessed | tf_op | source)
XLA Modules:
  0.0 71.5 jit_solution(17170746091235802962)
XLA Ops:
  0.6 52.7 %shard_map.110 = (f32[128,512]{1,0:T(8,128)S(1)}, f32[8,1024]{1,0:T(8,128)S(1)}, f32[8,1024]{1,0:T(8,128)S(1)}, f32[128,128]{1,0:T(8,128)S(1)}, f32[128,128]{1,0:T(8,128)S(1)}) custom-call(bf16[128,512]{1,0:T(8,128)(2,1)} %q_hbm.1, bf16[128,1024]{1,0:T(8,128)(2,1)} %rk_hbm.1, bf16[128,1024]{1,0:T(8,128)(2,1)} %rv_hbm.1, bf16[16,1024]{1,0:T(8,128)(2,1)} %pk_hbm.1, ...), custom_call_target="tpu_custom_call" | custom-call | flops 1426063360 | bytes 4194304 | tf_op jit(solution)/shard_map/pallas_call | solution.py:412
  53.3 0.0 copy-start
  53.3 0.7 copy-done
  54.0 0.0 copy-start.1
  54.0 0.6 copy-done.1
  54.6 0.0 copy-start.2
  54.6 0.6 copy-done.2
  55.3 0.0 copy-start.3
  55.3 0.6 copy-done.3
  55.9 0.0 copy-start.4
  55.9 0.6 copy-done.4
  56.5 15.0 %shard_map.111 = (f32[128,512]{1,0:T(8,128)}, f32[8,1024]{1,0:T(8,128)}, f32[8,1024]{1,0:T(8,128)}, f32[128,128]{1,0:T(8,128)}, f32[128,128]{1,0:T(8,128)}) custom-call(f32[128,512]{1,0:T(8,128)} %copy-done, f32[8,1024]{1,0:T(8,128)} %copy-done.3, f32[8,1024]{1,0:T(8,128)} %copy-done.4, f32[128,128]{1,0:T(8,128)} %copy-done.1, f32[128,128]{1,0:T(8,128)} %copy-done.2), custom_call_target="tpu_custom_call" | custom-call | tf_op jit(solution)/shard_map/pallas_call | solution.py:472
Async XLA Ops:
  53.3 0.7 copy-start
  54.0 0.6 copy-start.1
  54.6 0.6 copy-start.2
  55.3 0.6 copy-start.3
  55.9 0.6 copy-start.4

commit v4 on v3

--- a/solution.py
+++ b/solution.py
@@ -141,6 +141,7 @@
 
     offsets = [(i, j) for i in range(n_ring) for j in range(n_z) if i or j]
     offsets.sort(key=lambda o: -hops(o[0], n_ring) - hops(o[1], n_z))
+    classes = sorted(range(n_y), key=lambda v: -hops(v, n_ring) - hops(v + n_y, n_ring) - 8 * (v == 0) + 8 * (v == n_y // 2))
 
     barrier = pltpu.get_barrier_semaphore()
     for i, j in offsets:
@@ -160,16 +161,21 @@
     rows16 = pl.ds(pl.multiple_of(t * 16, 16), 16)
     spot = c * n_y + y
     for a in range(2):
-        for i, j in offsets:
-            to = tp_of[i] + zs[j]
-            rcopy(
-                pin.at[a, :, pl.ds(pl.multiple_of(to // 2 * HD, HD), HD)],
-                kv.at[a, spot, rows16],
-                a_send.at[a],
-                a_recv.at[a],
-                {"resp": resp_of[i], "tp": to},
-            ).start()
-        pltpu.make_async_copy(pin.at[a, :, pl.ds(col, HD)], kv.at[a, spot, rows16], a_recv.at[a]).start()
+        for v in classes:
+            for i, j in offsets:
+                if i % n_y == v:
+                    to = tp_of[i] + zs[j]
+                    rcopy(
+                        pin.at[a, :, pl.ds(pl.multiple_of(to // 2 * HD, HD), HD)],
+                        kv.at[a, spot, rows16],
+                        a_send.at[a],
+                        a_recv.at[a, v],
+                        {"resp": resp_of[i], "tp": to},
+                    ).start()
+            if v == 0:
+                pltpu.make_async_copy(
+                    pin.at[a, :, pl.ds(col, HD)], kv.at[a, spot, rows16], a_recv.at[a, 0]
+                ).start()
 
     for load in loads[2:]:
         load.wait()
@@ -187,21 +193,32 @@
     st_r[...] = s
     mx[...] = fold(s, jnp.max)
 
-    sends = []
+    sends, homes = [], []
 
     def start(copy):
         copy.start()
         sends.append(copy)
 
-    near = pl.ds(c * n_y, n_y)
-    far = pl.ds((1 - c) * n_y, n_y)
-
-    def gather(a):
-        pltpu.make_async_copy(kv.at[a, near], kv.at[a, near], a_recv.at[a]).wait()
-        start(rcopy(kv.at[a, near], kv.at[a, near], gs_send.at[a], gs_recv.at[a], sibling))
-
-    def gather_sib(a):
-        rcopy(kv.at[a, far], kv.at[a, far], gs_send.at[a], gs_recv.at[a], sibling).wait_recv()
+    def near(v):
+        return c * n_y + lax.rem(y + n_y - v, n_y)
+
+    def far(v):
+        return (1 - c) * n_y + lax.rem(y + n_y - v, n_y)
+
+    def gather(a, fn):
+        def from_sibling(v):
+            ref = kv.at[a, far(v)]
+            rcopy(ref, ref, gs_send.at[a, v], gs_recv.at[a, v], sibling).wait_recv()
+            fn(far(v))
+
+        for n, v in enumerate(classes):
+            ref = kv.at[a, near(v)]
+            pltpu.make_async_copy(ref, ref, a_recv.at[a, v]).wait()
+            start(rcopy(ref, ref, gs_send.at[a, v], gs_recv.at[a, v], sibling))
+            fn(near(v))
+            if n:
+                from_sibling(classes[n - 1])
+        from_sibling(classes[-1])
 
     def over(fn, first, blocks):
         lax.fori_loop(0, blocks, lambda i, carry: fn(first + i), None, unroll=UNROLL)
@@ -211,11 +228,7 @@
         st[b] = s
         mx[...] = jnp.maximum(mx[...], fold(s, jnp.max))
 
-    order = [k for k in (1, 3, 2) if k < n_y]
-    gather(0)
-    over(score, c * n_y, n_y)
-    gather_sib(0)
-    over(score, (1 - c) * n_y, n_y)
+    gather(0, score)
 
     mx[...] = jnp.broadcast_to(jnp.max(mx[...], axis=0, keepdims=True), mx.shape)
     def expo(x):
@@ -289,29 +302,20 @@
 
     def sum_y(a):
         total = acc[a, y, h]
-        for k in order:
+        for k in (1, 3, 2):
             rcopy(y_send.at[a, k], y_recv.at[a, k], fy_send.at[a, k], fy_recv.at[a, k], yline(k)).wait_recv()
             total = total + y_recv[a, k].astype(F32)
         p_send[a] = total.astype(BF16)
         home = rcopy(p_send.at[a], p_recv.at[a], fp_send.at[a], fp_recv.at[a], owner)
         local = pltpu.make_async_copy(p_send.at[a], p_recv.at[a], fp_recv.at[a])
-
-        @pl.when(away)
-        def _():
-            home.start()
-
-        @pl.when(r == g)
-        def _():
-            local.start()
-
-        return home
+        pl.when(away)(home.start)
+        pl.when(r == g)(local.start)
+        homes.append(home)
 
     p = times(st_r[...], sm[...]).astype(BF16)
     pb_r[...] = p
     rg_acc[1] = jnp.dot(p, do_s[...], preferred_element_type=F32)
     grad_pass(1, dv_block)
-    gather(1)
-
     d = jnp.dot(rkv[1], do_t[...], preferred_element_type=F32)
     dp_r[...] = d
     dl[...] = fold(pb_r[...].astype(F32) * d, jnp.sum)
@@ -321,12 +325,11 @@
         dp[b] = d
         dl[...] += fold(pb[b].astype(F32) * d, jnp.sum)
 
-    over(dprob, c * n_y, n_y)
+    gather(1, dprob)
     sum_z(1)
-    gather_sib(1)
-    over(dprob, (1 - c) * n_y, n_y)
     dl[...] = jnp.broadcast_to(jnp.sum(dl[...], axis=0, keepdims=True), dl.shape)
 
+    grad_pass(0, dk_block)
     ds = (times(st_r[...], sm[...]) * minus(dp_r[...], dl[...])).astype(BF16)
     pb_r[...] = ds
     rg_acc[0] = jnp.dot(ds, q_s[...], preferred_element_type=F32) * scale
@@ -344,8 +347,8 @@
     lax.fori_loop(1, n_tp, spread, 0)
     pltpu.make_async_copy(rg_send.at[t], rg_recv.at[t], rg_rsem.at[0]).start()
 
-    grad_pass(0, dk_block)
-    home_v = sum_y(1)
+
+    sum_y(1)
 
     def tdot(a, b):
         return lax.dot_general(a, b, (((0,), (0,)), ((), ())), preferred_element_type=F32)
@@ -362,10 +365,10 @@
         rdk_ref[:, i * HD : (i + 1) * HD] = both[:own_rows]
         rdv_ref[:, i * HD : (i + 1) * HD] = both[own_rows:]
 
-    home_k = sum_y(0)
-    home_v.wait_recv()
+    sum_y(0)
+    homes[0].wait_recv()
     pdv_ref[...] = p_recv[1].astype(F32)
-    home_k.wait_recv()
+    homes[1].wait_recv()
     pdk_ref[...] = p_recv[0].astype(F32)
 
     for a in range(2):
@@ -380,8 +383,8 @@
 
     @pl.when(away)
     def _():
-        home_v.wait_send()
-        home_k.wait_send()
+        for home in homes:
+            home.wait_send()
 
 
 def write_out(*refs):
@@ -446,9 +449,9 @@
                 vmem((n_resp * n_tp // 2, 16, HD), BF16),
                 dma((4 + 2 * heads,)),
                 dma((2,)),
-                dma((2,)),
-                dma((2,)),
-                dma((2,)),
+                dma((2, n_y)),
+                dma((2, n_y)),
+                dma((2, n_y)),
                 dma((2, n_y)),
                 dma((2, n_y)),
                 dma((2, n_y)),
@@ -475,6 +478,7 @@
             in_specs=[any_spec] * 5,
             out_specs=(any_spec,) * 5,
             scratch_shapes=[dma((5,))],
+            compiler_params=pltpu.CompilerParams(vmem_limit_bytes=256 * 1024),
         )(*results)
 
     return jax.shard_map(

time: 71.7 us -> 52.6 us (0.73)
  the two profiles are of different devices: /device:TPU:46 before, /device:TPU:1 now
where the time goes in v4:
time: 52.6 us; the launch traced here: 52.1 us
  Pallas kernels  51.4 us (98%)
  between operations  0.64 us (1%)
    pallas_call x1, Pallas kernels, per_device(): pl.pallas_call(functools.partial(kernel, n_resp, n_tp), out_shape=tuple((...  50.6 us

profile of v4, /device:TPU:1, one launch (start us, length us, event | category | flops | bytes accessed | tf_op | source)
XLA Modules:
  0.0 52.1 jit_solution(10371540187038221055)
XLA Ops:
  0.6 50.6 %shard_map.110 = (f32[128,512]{1,0:T(8,128)S(1)}, f32[8,1024]{1,0:T(8,128)S(1)}, f32[8,1024]{1,0:T(8,128)S(1)}, f32[128,128]{1,0:T(8,128)S(1)}, f32[128,128]{1,0:T(8,128)S(1)}) custom-call(bf16[128,512]{1,0:T(8,128)(2,1)} %q_hbm.1, bf16[128,1024]{1,0:T(8,128)(2,1)} %rk_hbm.1, bf16[128,1024]{1,0:T(8,128)(2,1)} %rv_hbm.1, bf16[16,1024]{1,0:T(8,128)(2,1)} %pk_hbm.1, ...), custom_call_target="tpu_custom_call" | custom-call | flops 1426063360 | bytes 4194304 | tf_op jit(solution)/shard_map/pallas_call | solution.py:415
  51.2 0.8 %shard_map.111 = (f32[128,512]{1,0:T(8,128)}, f32[8,1024]{1,0:T(8,128)}, f32[8,1024]{1,0:T(8,128)}, f32[128,128]{1,0:T(8,128)}, f32[128,128]{1,0:T(8,128)}) custom-call(f32[128,512]{1,0:T(8,128)S(1)} %get-tuple-element.10.refs_0_, f32[8,1024]{1,0:T(8,128)S(1)} %get-tuple-element.11.refs_1_, f32[8,1024]{1,0:T(8,128)S(1)} %get-tuple-element.12.refs_2_, ...), custom_call_target="tpu_custom_call" | custom-call | tf_op jit(solution)/shard_map/pallas_call | solution.py:475

commit v5 on v4

v5 whole, which is shorter than its diff:
```python
import functools
import math

import jax
import jax.numpy as jnp
from jax import lax
from jax.experimental import pallas as pl
from jax.experimental.pallas import tpu as pltpu
from jax.sharding import PartitionSpec as P

MESH = pl.DeviceIdType.MESH
HD = 128
TILE = 16
F32 = jnp.float32
BF16 = jnp.bfloat16


def flip(value, bits):
    if bits & 1:
        value = value + 1 - 2 * lax.rem(value, 2)
    if bits & 2:
        value = value + 2 - 4 * lax.rem(value // 2, 2)
    return value


def fold(x, op):
    return op(x.reshape(x.shape[0] // 8, 8, x.shape[1]), axis=0)


def by_row(x, v, op):
    return op(x.reshape(x.shape[0] // 8, 8, x.shape[1]), v[None]).reshape(x.shape)


def kernel(
    n_resp,
    n_tp,
    q_hbm,
    rk_hbm,
    rv_hbm,
    pk_hbm,
    pv_hbm,
    ct_hbm,
    len_ref,
    dq_ref,
    rdk_ref,
    rdv_ref,
    pdk_ref,
    pdv_ref,
    pin,
    kv,
    rkv,
    qd,
    qd_t,
    st,
    dp,
    pb,
    st_r,
    dp_r,
    pb_r,
    mx,
    sm,
    dl,
    stat_send,
    stat_recv,
    del_send,
    del_recv,
    acc,
    y_send,
    y_recv,
    p_send,
    p_recv,
    rg_send,
    rg_recv,
    rg_acc,
    dqs_send,
    dqs_recv,
    dqz_send,
    dqz_recv,
    sent,
    in_sem,
    a_send,
    a_recv,
    xq_send,
    xq_recv,
    st_ssem,
    st_rsem,
    de_ssem,
    de_rsem,
    fy_send,
    fy_recv,
    fp_send,
    fp_recv,
    rg_ssem,
    rg_rsem,
    dq_ssem,
    dq_rsem,
):
    r = lax.axis_index("resp")
    t = lax.axis_index("tp")
    n_y = n_resp // 2
    n_z = n_tp // 2
    n_ring = 2 * n_y
    y, c = r // 2, lax.rem(r, 2)
    g, h = t // 2, lax.rem(t, 2)
    y_hi, z = t // n_z, lax.rem(t, n_z)
    count = q_hbm.shape[0]
    heads = q_hbm.shape[1] // HD
    rows = heads * count
    scale = 1.0 / math.sqrt(HD)

    def rcopy(src, dst, send, recv, dev):
        return pltpu.make_async_remote_copy(
            src_ref=src, dst_ref=dst, send_sem=send, recv_sem=recv, device_id=dev, device_id_type=MESH
        )

    sends = []

    def start(copy):
        copy.start()
        sends.append(copy)

    def mate(m):
        return {"resp": flip(r, m & 1), "tp": flip(t, m >> 1)}

    def yline(k):
        return {"resp": 2 * flip(y, k) + c, "tp": t}

    def owner(k):
        return {"resp": g, "tp": 2 * r + k}

    def own(k):
        return jnp.logical_and(r == g, h == k)

    ys = [lax.rem(y_hi * n_y + y + d, n_ring) for d in range(n_ring)]
    resp_of = [2 * lax.rem(v, n_y) + c for v in ys]
    tp_of = [v // n_y * n_z for v in ys]
    sign = 1 - 2 * h
    z_to = [lax.rem(z + sign * d + n_z, n_z) for d in (0, -1, 2, -3)]
    z_from = [lax.rem(z - sign * d + n_z, n_z) for d in range(4)]

    def hops(d):
        return min(d, n_ring - d)

    offsets = [(i, j) for i in range(n_ring) for j in range(4) if i or j]
    offsets.sort(key=lambda o: -hops(o[0]) - o[1])
    classes = (0, 1, 3, 2)

    barrier = pltpu.get_barrier_semaphore()
    for i, j in offsets:
        pl.semaphore_signal(
            barrier, inc=1, device_id={"resp": resp_of[i], "tp": tp_of[i] + z_from[j]}, device_id_type=MESH
        )

    def greet(d, carry):
        pl.semaphore_signal(
            barrier, inc=1, device_id={"resp": r, "tp": lax.rem(t + d, n_tp)}, device_id_type=MESH
        )
        return carry

    lax.fori_loop(1, n_tp, greet, 0)
    for m in (1, 3):
        pl.semaphore_signal(barrier, inc=1, device_id=mate(m), device_id_type=MESH)
    for k in range(2):

        @pl.when(jnp.logical_not(own(k)))
        def _(k=k):
            pl.semaphore_signal(barrier, inc=1, device_id=owner(k), device_id_type=MESH)

    col = pl.multiple_of(g * HD, HD)
    loads = [
        pltpu.make_async_copy(pk_hbm, pin.at[0], in_sem.at[0]),
        pltpu.make_async_copy(pv_hbm, pin.at[1], in_sem.at[1]),
        pltpu.make_async_copy(rk_hbm.at[:, pl.ds(col, HD)], rkv.at[0], in_sem.at[2]),
        pltpu.make_async_copy(rv_hbm.at[:, pl.ds(col, HD)], rkv.at[1], in_sem.at[3]),
    ]
    for i, ref in enumerate((q_hbm, ct_hbm)):
        for j in range(heads):
            loads.append(
                pltpu.make_async_copy(
                    ref.at[:, pl.ds(j * HD, HD)], qd.at[i, 0, pl.ds(j * count, count)], in_sem.at[4 + heads * i + j]
                )
            )
    for load in loads:
        load.start()
    loads[0].wait()
    for load in loads[4 : 4 + heads]:
        load.wait()
    same = (r == g).astype(jnp.int32)
    pl.semaphore_wait(barrier, len(offsets) + n_tp - 1 + 2 + 2 - same)

    def share(i):
        for m in (2, 1):
            start(rcopy(qd.at[i, 0], qd.at[i, m], xq_send.at[i, m], xq_recv.at[i, m], mate(m)))

    def shared(i, m):
        rcopy(qd.at[i, m], qd.at[i, m], xq_send.at[i, m], xq_recv.at[i, m], mate(m)).wait_recv()

    def relay(i):
        shared(i, 2)
        start(rcopy(qd.at[i, 2], qd.at[i, 3], xq_send.at[i, 3], xq_recv.at[i, 3], mate(1)))

    def turn(i, m):
        qd_t[i, m] = jnp.transpose(qd[i, m].astype(F32)).astype(BF16)

    def scatter(a):
        for v in classes:
            for i, j in [o for o in offsets if o[0] % n_y == v] + [(0, 0)] * (v == 0):
                to = tp_of[i] + z_to[j]
                slot = pl.ds(pl.multiple_of(y_hi * 4 * TILE + j * TILE, TILE), TILE)
                src = pin.at[a, :, pl.ds(pl.multiple_of(to // 2 * HD, HD), HD)]
                dst = kv.at[a, y, slot]
                if i or j:
                    rcopy(src, dst, a_send.at[a], a_recv.at[a, v], {"resp": resp_of[i], "tp": to}).start()
                else:
                    pltpu.make_async_copy(src, dst, a_recv.at[a, v]).start()

    share(0)
    scatter(0)
    for load in loads[4 + heads :]:
        load.wait()
    length = len_ref[r]
    live = lax.rem(lax.broadcasted_iota(jnp.int32, (rows, HD), 0), count) < length
    qd[1, 0] = jnp.where(live, qd[1, 0].astype(F32), 0.0).astype(BF16)
    share(1)
    for load in loads[1:4]:
        load.wait()
    scatter(1)

    turn(0, 0)
    s = jnp.dot(rkv[0], qd_t[0, 0], preferred_element_type=F32) * scale
    key_pos = lax.broadcasted_iota(jnp.int32, s.shape, 0)
    row_pos = lax.rem(lax.broadcasted_iota(jnp.int32, s.shape, 1), count)
    s = jnp.where(key_pos <= row_pos, s, -jnp.inf)
    st_r[...] = s
    mx[0] = fold(s, jnp.max)
    for m in range(1, 4):
        mx[m] = jnp.full((8, rows), -jnp.inf, F32)
    turn(1, 0)

    relay(0)
    turn(0, 2)
    shared(0, 1)
    turn(0, 1)
    shared(0, 3)
    turn(0, 3)

    def arrived(a, v):
        b = lax.rem(y + n_y - v, n_y)
        pltpu.make_async_copy(kv.at[a, b], kv.at[a, b], a_recv.at[a, v]).wait()
        return b

    for n, v in enumerate(classes):
        b = arrived(0, v)
        for m in range(4):
            s = jnp.dot(kv[0, b], qd_t[0, m], preferred_element_type=F32) * scale
            st[b, m] = s
            mx[m] = jnp.maximum(mx[m], fold(s, jnp.max))
        if n == 0:
            relay(1)

    for m in range(4):
        top = jnp.max(mx[m], axis=0, keepdims=True)
        stat_send[0, m] = top
        mx[m] = jnp.broadcast_to(top, (8, rows))
    e = jnp.exp(by_row(st_r[...], mx[0], jnp.subtract))
    st_r[...] = e
    sm[0] = fold(e, jnp.sum)
    for m in range(1, 4):
        sm[m] = jnp.zeros((8, rows), F32)

    def soften(b, carry):
        for m in range(4):
            e = jnp.exp(by_row(st[b, m], mx[m], jnp.subtract))
            st[b, m] = e
            sm[m] += fold(e, jnp.sum)
        return carry

    lax.fori_loop(0, n_y, soften, 0, unroll=True)
    for m in range(4):
        stat_send[1, m] = jnp.sum(sm[m], axis=0, keepdims=True)
    for p in (2, 3, 1):
        start(rcopy(stat_send, stat_recv.at[p], st_ssem.at[p], st_rsem.at[p], mate(p)))
    turn(1, 2)
    shared(1, 1)
    turn(1, 1)
    shared(1, 3)
    turn(1, 3)
    for p in (1, 2, 3):
        rcopy(stat_send, stat_recv.at[p], st_ssem.at[p], st_rsem.at[p], mate(p)).wait_recv()
    for m in range(4):
        tops = [stat_send[0, m]] + [stat_recv[p, 0, m ^ p] for p in (1, 2, 3)]
        sums = [stat_send[1, m]] + [stat_recv[p, 1, m ^ p] for p in (1, 2, 3)]
        top = functools.reduce(jnp.maximum, tops)
        parts = [jnp.exp(v - top) for v in tops]
        total = sum(u * v for u, v in zip(parts, sums))
        sm[m] = jnp.broadcast_to(parts[0] / total, (8, rows))

    def to_y(a, k, value):
        if k:
            y_send[a, k] = value.astype(BF16)
            start(rcopy(y_send.at[a, k], y_recv.at[a, k], fy_send.at[a, k], fy_recv.at[a, k], yline(k)))
        else:
            acc[a] = value

    p = by_row(st_r[...], sm[0], jnp.multiply).astype(BF16)
    pb_r[...] = p
    for k in (3, 2, 1, 0):
        b = flip(y, k)
        for m in range(4):
            pb[b, :, m * rows : (m + 1) * rows] = by_row(st[b, m], sm[m], jnp.multiply).astype(BF16)
        to_y(1, k, jnp.dot(pb[b], qd[1].reshape(4 * rows, HD), preferred_element_type=F32))
    rg_acc[1] = jnp.dot(p, qd[1, 0], preferred_element_type=F32)

    d = jnp.dot(rkv[1], qd_t[1, 0], preferred_element_type=F32)
    dp_r[...] = d
    dl[0] = fold(pb_r[...].astype(F32) * d, jnp.sum)
    for m in range(1, 4):
        dl[m] = jnp.zeros((8, rows), F32)
    for v in classes:
        b = arrived(1, v)
        for m in range(4):
            d = jnp.dot(kv[1, b], qd_t[1, m], preferred_element_type=F32)
            dp[b, m] = d
            dl[m] += fold(pb[b, :, m * rows : (m + 1) * rows].astype(F32) * d, jnp.sum)
    for m in range(4):
        del_send[m] = jnp.sum(dl[m], axis=0, keepdims=True)
    for p in (2, 3, 1):
        start(rcopy(del_send, del_recv.at[p], de_ssem.at[p], de_rsem.at[p], mate(p)))

    def sum_y(a):
        total = acc[a]
        for k in (1, 3, 2):
            rcopy(y_send.at[a, k], y_recv.at[a, k], fy_send.at[a, k], fy_recv.at[a, k], yline(k)).wait_recv()
            total = total + y_recv[a, k].astype(F32)
        p_send[a] = total.astype(BF16).reshape(2, 4 * TILE, HD)
        for k in range(2):
            home = rcopy(p_send.at[a, k], p_recv.at[a, h], fp_send.at[a, k], fp_recv.at[a, h], owner(k))
            local = pltpu.make_async_copy(p_send.at[a, k], p_recv.at[a, h], fp_recv.at[a, h])
            pl.when(jnp.logical_not(own(k)))(home.start)
            pl.when(own(k))(local.start)

    for p in (1, 2, 3):
        rcopy(del_send, del_recv.at[p], de_ssem.at[p], de_rsem.at[p], mate(p)).wait_recv()
    for m in range(4):
        total = del_send[m] + del_recv[1, m ^ 1] + del_recv[2, m ^ 2] + del_recv[3, m ^ 3]
        dl[m] = jnp.broadcast_to(total, (8, rows))

    def d_score(e, d, m):
        return (by_row(e, sm[m], jnp.multiply) * by_row(d, dl[m], jnp.subtract)).astype(BF16)

    for k in (3, 2, 1, 0):
        b = flip(y, k)
        for m in range(4):
            pb[b, :, m * rows : (m + 1) * rows] = d_score(st[b, m], dp[b, m], m)
        to_y(0, k, jnp.dot(pb[b], qd[0].reshape(4 * rows, HD), preferred_element_type=F32) * scale)
    ds = d_score(st_r[...], dp_r[...], 0)
    pb_r[...] = ds
    rg_acc[0] = jnp.dot(ds, qd[0, 0], preferred_element_type=F32) * scale
    own_rows = count // n_tp
    rg = jnp.concatenate(
        [rg_acc[0].reshape(n_tp, own_rows, HD), rg_acc[1].reshape(n_tp, own_rows, HD)], axis=1
    )
    rg_send[...] = rg.astype(BF16)

    def spread(d, carry):
        to = lax.rem(t + d, n_tp)
        rcopy(rg_send.at[to], rg_recv.at[t], rg_ssem.at[0], rg_rsem.at[0], {"resp": r, "tp": to}).start()
        return carry

    lax.fori_loop(1, n_tp, spread, 0)
    pltpu.make_async_copy(rg_send.at[t], rg_recv.at[t], rg_rsem.at[0]).start()

    def tdot(a, b):
        return lax.dot_general(a, b, (((0,), (0,)), ((), ())), preferred_element_type=F32)

    keys = kv[0].reshape(n_y * 8 * TILE, HD)

    def dq_part(m):
        return tdot(keys, pb[:, :, m * rows : (m + 1) * rows].reshape(n_y * 8 * TILE, rows))

    dqs_send[0] = dq_part(1).astype(BF16)
    dqs_send[1] = dq_part(3).astype(BF16)
    start(rcopy(dqs_send, dqs_recv, dq_ssem.at[0], dq_rsem.at[0], mate(1)))
    there = dq_part(2)
    rcopy(dqs_send, dqs_recv, dq_ssem.at[0], dq_rsem.at[0], mate(1)).wait_recv()
    dqz_send[...] = (there + dqs_recv[1].astype(F32)).astype(BF16)
    start(rcopy(dqz_send, dqz_recv, dq_ssem.at[1], dq_rsem.at[1], mate(2)))
    sum_y(1)
    dq_t = dq_part(0) + tdot(rkv[0], pb_r[...]) + dqs_recv[0].astype(F32)
    sum_y(0)
    rcopy(dqz_send, dqz_recv, dq_ssem.at[1], dq_rsem.at[1], mate(2)).wait_recv()
    dq_t = dq_t + dqz_recv[...].astype(F32)
    for j in range(heads):
        dq_ref[:, j * HD : (j + 1) * HD] = jnp.transpose(dq_t[:, j * count : (j + 1) * count]) * scale

    pltpu.make_async_copy(rg_recv, rg_recv, rg_rsem.at[0]).wait()
    got = rg_recv[...].astype(F32)
    for i in range(n_tp // 2):
        both = got[2 * i] + got[2 * i + 1]
        rdk_ref[:, i * HD : (i + 1) * HD] = both[:own_rows]
        rdv_ref[:, i * HD : (i + 1) * HD] = both[own_rows:]

    first = 2 * lax.rem(r, n_z // 2)
    for a, ref in ((1, pdv_ref), (0, pdk_ref)):
        for i in range(2):
            got = p_recv.at[a, i]
            rcopy(got, got, fp_send.at[a, i], fp_recv.at[a, i], mate(1)).wait_recv()
            for d in range(4):
                at = lax.rem(first + n_z - d, n_z) if i == 0 else lax.rem(first + 1 + d, n_z)
                ref[pl.ds(pl.multiple_of(at * TILE, TILE), TILE)] = got[d * TILE : (d + 1) * TILE].astype(F32)

    for a in range(2):
        out = sent.at[pl.ds(0, len(offsets))]
        pltpu.make_async_copy(out, out, a_send.at[a]).wait()
    out = rg_send.at[pl.ds(0, n_tp - 1)]
    pltpu.make_async_copy(out, out, rg_ssem.at[0]).wait()
    for copy in sends:
        copy.wait_send()
    for a in range(2):
        for k in range(2):
            home = rcopy(p_send.at[a, k], p_recv.at[a, h], fp_send.at[a, k], fp_recv.at[a, h], owner(k))
            pl.when(jnp.logical_not(own(k)))(home.wait_send)


def write_out(*refs):
    sem = refs[10]
    copies = [pltpu.make_async_copy(refs[i], refs[5 + i], sem.at[i]) for i in range(5)]
    for copy in copies:
        copy.start()
    for copy in copies:
        copy.wait()


def solution(mesh):
    n_resp, n_tp = mesh.shape["resp"], mesh.shape["tp"]
    n_y = n_resp // 2

    def per_device(queries, resp_keys, resp_values, prefix_keys, prefix_values, cotangent, lengths):
        count, width = queries.shape
        heads = width // HD
        rows = heads * count
        half = n_tp // 2 * TILE
        cols = prefix_keys.shape[1]
        dma = pltpu.SemaphoreType.DMA
        vmem = pltpu.VMEM
        any_spec = pl.BlockSpec(memory_space=pl.ANY)
        vmem_spec = pl.BlockSpec(memory_space=pltpu.VMEM)
        shapes = ((count, width), (count // n_tp, cols), (count // n_tp, cols), (half, HD), (half, HD))
        results = pl.pallas_call(
            functools.partial(kernel, n_resp, n_tp),
            out_shape=tuple(pltpu.VMEM(shape, F32) for shape in shapes),
            in_specs=[any_spec] * 6 + [pl.BlockSpec(memory_space=pltpu.SMEM)],
            out_specs=(vmem_spec,) * 5,
            scratch_shapes=[
                vmem((2, TILE, cols), BF16),
                vmem((2, n_y, half, HD), BF16),
                vmem((2, count, HD), BF16),
                vmem((2, 4, rows, HD), BF16),
                vmem((2, 4, HD, rows), BF16),
                vmem((n_y, 4, half, rows), F32),
                vmem((n_y, 4, half, rows), F32),
                vmem((n_y, half, 4 * rows), BF16),
                vmem((count, rows), F32),
                vmem((count, rows), F32),
                vmem((count, rows), BF16),
                vmem((4, 8, rows), F32),
                vmem((4, 8, rows), F32),
                vmem((4, 8, rows), F32),
                vmem((2, 4, 1, rows), F32),
                vmem((4, 2, 4, 1, rows), F32),
                vmem((4, 1, rows), F32),
                vmem((4, 4, 1, rows), F32),
                vmem((2, half, HD), F32),
                vmem((2, n_y, half, HD), BF16),
                vmem((2, n_y, half, HD), BF16),
                vmem((2, 2, half // 2, HD), BF16),
                vmem((2, 2, half // 2, HD), BF16),
                vmem((n_tp, 16, HD), BF16),
                vmem((n_tp, 16, HD), BF16),
                vmem((2, count, HD), F32),
                vmem((2, HD, rows), BF16),
                vmem((2, HD, rows), BF16),
                vmem((HD, rows), BF16),
                vmem((HD, rows), BF16),
                vmem((n_resp * 4, TILE, HD), BF16),
                dma((4 + 2 * heads,)),
                dma((2,)),
                dma((2, n_y)),
                dma((2, 4)),
                dma((2, 4)),
                dma((4,)),
                dma((4,)),
                dma((4,)),
                dma((4,)),
                dma((2, n_y)),
                dma((2, n_y)),
                dma((2, 2)),
                dma((2, 2)),
                dma((1,)),
                dma((1,)),
                dma((2,)),
                dma((2,)),
            ],
            compiler_params=pltpu.CompilerParams(
                collective_id=0, has_side_effects=True, vmem_limit_bytes=62 * 1024 * 1024
            ),
            cost_estimate=pl.CostEstimate(
                flops=10 * rows * (n_resp * 2 * half + count) * HD,
                bytes_accessed=4 * 1024 * 1024,
                transcendentals=rows * (n_resp * 2 * half + count),
            ),
        )(queries, resp_keys, resp_values, prefix_keys, prefix_values, cotangent, lengths)
        return pl.pallas_call(
            write_out,
            out_shape=tuple(jax.ShapeDtypeStruct(shape, F32) for shape in shapes),
            in_specs=[any_spec] * 5,
            out_specs=(any_spec,) * 5,
            scratch_shapes=[dma((5,))],
            compiler_params=pltpu.CompilerParams(vmem_limit_bytes=256 * 1024),
        )(*results)

    return jax.shard_map(
        per_device,
        mesh=mesh,
        in_specs=(
            P(("grp", "resp"), "tp"),
            P(("grp", "resp"), None),
            P(("grp", "resp"), None),
            P(("grp", "resp", "tp"), None),
            P(("grp", "resp", "tp"), None),
            P(("grp", "resp"), "tp"),
            P("grp"),
        ),
        out_specs=(
            P(("grp", "resp"), "tp"),
            P(("grp", "resp", "tp"), None),
            P(("grp", "resp", "tp"), None),
            P(("grp", "tp"), "resp"),
            P(("grp", "tp"), "resp"),
        ),
        check_vma=False,
    )
```

time: 52.6 us -> 50.1 us (0.952)
  Pallas kernels: 51.4 us -> 49.2 us
    pallas_call x1, Pallas kernels: 50.6 us -> 48.4 us  [per_device(): pl.pallas_call(functools.partial(kernel, n_resp, n_tp), out_shape=tuple((...]
where the time goes in v5:
time: 50.1 us; the launch traced here: 49.8 us
  Pallas kernels  49.2 us (98%)
  between operations  0.64 us (1%)
    pallas_call x1, Pallas kernels, per_device(): pl.pallas_call(functools.partial(kernel, n_resp, n_tp), out_shape=tuple((...  48.4 us

profile of v5, /device:TPU:1, one launch (start us, length us, event | category | flops | bytes accessed | tf_op | source)
XLA Modules:
  0.0 49.8 jit_solution(8200998245115740061)
XLA Ops:
  0.6 48.4 %shard_map.110 = (f32[128,512]{1,0:T(8,128)S(1)}, f32[8,1024]{1,0:T(8,128)S(1)}, f32[8,1024]{1,0:T(8,128)S(1)}, f32[128,128]{1,0:T(8,128)S(1)}, f32[128,128]{1,0:T(8,128)S(1)}) custom-call(bf16[128,512]{1,0:T(8,128)(2,1)} %q_hbm.1, bf16[128,1024]{1,0:T(8,128)(2,1)} %rk_hbm.1, bf16[128,1024]{1,0:T(8,128)(2,1)} %rv_hbm.1, bf16[16,1024]{1,0:T(8,128)(2,1)} %pk_hbm.1, ...), custom_call_target="tpu_custom_call" | custom-call | flops 1426063360 | bytes 4194304 | tf_op jit(solution)/shard_map/pallas_call | solution.py:449
  49.0 0.8 %shard_map.111 = (f32[128,512]{1,0:T(8,128)}, f32[8,1024]{1,0:T(8,128)}, f32[8,1024]{1,0:T(8,128)}, f32[128,128]{1,0:T(8,128)}, f32[128,128]{1,0:T(8,128)}) custom-call(f32[128,512]{1,0:T(8,128)S(1)} %get-tuple-element.10.refs_0_, f32[8,1024]{1,0:T(8,128)S(1)} %get-tuple-element.11.refs_1_, f32[8,1024]{1,0:T(8,128)S(1)} %get-tuple-element.12.refs_2_, ...), custom_call_target="tpu_custom_call" | custom-call | tf_op jit(solution)/shard_map/pallas_call | solution.py:513
